TPU v7x, 32 devices: a whole 2x2x4 slice. The times are simulated.
32 devices in a mesh: dp: 16 (over z, y, x), mp: 2 (over core).
Axes of the slice: x: 2, y: 2, z: 4, core: 2. Of those that a mesh axis runs over, the one named last changes fastest.
Arguments:
- tokens: bfloat16 [15760, 768], P('dp'), may hold values from -6 to 6
- ln1_gain: bfloat16 [768], P('dp'), may hold values from 0.5 to 1.5
- w_qkv: bfloat16 [768, 3, 768], P('dp', None, 'mp'), may hold values from -0.21875 to 0.21875
- w_out: bfloat16 [768, 768], P('mp', 'dp'), may hold values from -0.625 to 0.625
- out_bias: bfloat16 [768], P('dp'), may hold values from -3 to 3
- ln2_gain: bfloat16 [768], P('dp'), may hold values from 0.5 to 1.5
- router: bfloat16 [768, 16], P('dp'), may hold values from -0.15625 to 0.15625
- w_in: bfloat16 [16, 768, 3072], P('dp', None, 'mp'), may hold values from -0.21875 to 0.21875
- in_bias: bfloat16 [16, 3072], P('dp', 'mp'), may hold values from -3 to 3
- w_back: bfloat16 [16, 3072, 768], P('dp', 'mp'), may hold values from -0.875 to 0.875
- back_bias: bfloat16 [16, 768], P('dp'), may hold values from -4 to 4
- routes: int32 [15760, 2], P('dp'), may hold values from 0 to 15, all different within a row; in each aligned block of 985 rows (0 to 984, 985 to 1969, ...) at most 306 rows name the same one
- priority: int32 [16, 985], P('dp'), may hold values from 0 to 984, each once within a row
- cotangent: bfloat16 [15760, 768], P('dp'), may hold values from -6 to 6
Outputs:
- output: bfloat16 [15760, 768], P('dp')
- token_gradient: bfloat16 [15760, 768], P('dp')
- grad_ln1_gain: float32 [768], P('dp')
- grad_w_qkv: float32 [768, 3, 768], P('dp', None, 'mp')
- grad_w_out: float32 [768, 768], P('mp', 'dp')
- grad_out_bias: float32 [768], P('dp')
- grad_ln2_gain: float32 [768], P('dp')
- grad_router: float32 [768, 16], P('dp')
- grad_w_in: float32 [16, 768, 3072], P('dp', None, 'mp')
- grad_in_bias: float32 [16, 3072], P('dp', 'mp')
- grad_w_back: float32 [16, 3072, 768], P('dp', 'mp')
- grad_back_bias: float32 [16, 768], P('dp')
Inputs may be any that keep to these rules, and one draw needn't show every extreme that they name: `routes`: in the rows of one index of dp no expert is named by more than 306 rows; a row never names one expert twice. `priority`: each row orders the 985 tokens of its group, each rank once.
All inputs are finite; a program needn't handle non-finite values.
Results may differ from a plain program's by a relative error of at most 0.017.
Values may be sent and summed in bfloat16 or wider, within the bound.
A program may use at most 192 MiB of HBM per device.

v0:
```python
from functools import partial

import jax
import jax.numpy as jnp
from jax import lax
from jax.sharding import PartitionSpec as P

D = 768
HD = 64
SEQ = 197


epsilon = 1e-06


def routing(route_rows, ranking, experts, capacity):
    tok_rows = route_rows.shape[0]
    ranked = jnp.arange(2, dtype=jnp.int32)[None, :] * tok_rows + ranking[:, None]
    by_order = (
        jnp.zeros((2 * tok_rows,), jnp.int32).at[ranked.reshape(-1)].set(route_rows.reshape(-1))
    )
    onehot = (by_order[:, None] == jnp.arange(experts, dtype=jnp.int32)[None, :]).astype(jnp.int32)
    earlier = jnp.cumsum(onehot, axis=0, dtype=jnp.int32) - onehot
    slot_of = jnp.sum(earlier * onehot, axis=1, dtype=jnp.int32)
    slot_ids = slot_of[ranked]
    return jnp.where(slot_ids < capacity, route_rows * capacity + slot_ids, experts * capacity)


def pair_of_slot(slot_index, experts, capacity):
    pair_count = slot_index.shape[0] * slot_index.shape[1]
    empty = jnp.full((experts * capacity,), pair_count, jnp.int32)
    return empty.at[slot_index.reshape(-1)].set(
        jnp.arange(pair_count, dtype=jnp.int32), mode="drop"
    )


def apply_norm(values):
    average = jnp.mean(values, axis=-1, keepdims=True)
    centered = values - average
    row_inverse_deviation = lax.rsqrt(
        jnp.mean(centered * centered, axis=-1, keepdims=True) + epsilon
    )
    return (centered * row_inverse_deviation, row_inverse_deviation)


def norm_backward(norm_gradient, scale_factor, standardized_rows, row_inverse_deviation):
    standardized_gradient = norm_gradient * scale_factor[None, :]
    return row_inverse_deviation * (
        standardized_gradient
        - jnp.mean(standardized_gradient, axis=-1, keepdims=True)
        - standardized_rows
        * jnp.mean(standardized_gradient * standardized_rows, axis=-1, keepdims=True)
    )


def contract_last(left, right):
    return lax.dot_general(
        left, right, (((1,), (1,)), ((), ())), preferred_element_type=jnp.float32
    )


def contract_first(left, right):
    return lax.dot_general(
        left, right, (((0,), (0,)), ((), ())), preferred_element_type=jnp.float32
    )


def across_half(values):
    return lax.all_to_all(values, "dp", split_axis=0, concat_axis=0, tiled=True)


def join_columns(values):
    return lax.all_gather(values, "mp", axis=2, tiled=True)


def to_experts(buffer):
    col_width = buffer.shape[2] // lax.axis_size("mp")
    own_cols = lax.dynamic_slice_in_dim(buffer, lax.axis_index("mp") * col_width, col_width, 2)
    gathered = join_columns(across_half(own_cols))
    return gathered.reshape(-1, gathered.shape[2])


def from_experts(partial_sum, bias_row):
    groups = lax.axis_size("dp")
    shared = lax.psum_scatter(partial_sum, "mp", scatter_dimension=1, tiled=True)
    col_width = shared.shape[1]
    bias_part = lax.dynamic_slice_in_dim(bias_row, lax.axis_index("mp") * col_width, col_width, 0)
    out_rows = (shared + bias_part[None, :]).astype(jnp.bfloat16).reshape(groups, -1, col_width)
    at_home = join_columns(across_half(out_rows))
    return at_home.reshape(-1, at_home.shape[2])


def body(
    tokens,
    ln1_gain,
    w_qkv,
    w_out,
    out_bias,
    ln2_gain,
    router,
    w_in,
    in_bias,
    w_back,
    back_bias,
    routes,
    priority,
    cotangent,
):
    tok_rows = tokens.shape[0]
    images = tok_rows // SEQ
    local_width = w_qkv.shape[2]
    local_heads = local_width // HD
    experts = router.shape[1]
    capacity = max(2, 5 * tok_rows // (2 * experts))
    score_scale = HD ** (-0.5)
    input_tokens = tokens.astype(jnp.float32)
    first_standardized, first_inverse_deviation = apply_norm(input_tokens)
    qkv_init = jnp.zeros((1, 1, 1), jnp.bfloat16)
    qkv_all = qkv_init
    part_qkv = lax.all_gather(w_qkv, "dp", axis=0, tiled=True)
    part_one = lax.all_gather(ln1_gain, "dp", axis=0, tiled=True)
    part_two = lax.all_gather(ln2_gain, "dp", axis=0, tiled=True)
    part_bias = lax.all_gather(out_bias, "dp", axis=0, tiled=True)
    part_router = lax.all_gather(router, "dp", axis=0, tiled=True)
    row_count = part_qkv.shape[0]
    column_total = first_standardized
    normed = (column_total * part_one.astype(jnp.float32)[None, :]).astype(jnp.bfloat16)
    merged_sum = jnp.dot(
        normed, part_qkv.reshape(row_count, -1), preferred_element_type=jnp.float32
    )
    gain_one = part_one
    gain_two = part_two
    bias_out = part_bias
    router_all = part_router
    merged_sum, gain_one, gain_two, bias_out, router_all, qkv_all = (
        merged_sum,
        gain_one,
        gain_two,
        bias_out,
        router_all,
        qkv_all,
    )
    first_gain_f32 = gain_one.astype(jnp.float32)
    second_gain_f32 = gain_two.astype(jnp.float32)
    first_normalized = (first_standardized * first_gain_f32[None, :]).astype(jnp.bfloat16)
    merged_low = merged_sum.astype(jnp.bfloat16).reshape(images, SEQ, 3, local_heads, HD)
    queries = merged_low[:, :, 0]
    keys_all = merged_low[:, :, 1]
    values_all = merged_low[:, :, 2]
    scores = (
        jnp.einsum("bqhd,bkhd->bhqk", queries, keys_all, preferred_element_type=jnp.float32)
        * score_scale
    )
    row_max = jnp.max(scores, axis=-1, keepdims=True)
    raised = jnp.exp(scores - row_max)
    summed = jnp.sum(raised, axis=-1, keepdims=True)
    weights = raised / summed
    log_total = row_max + jnp.log(summed)
    attended = jnp.einsum(
        "bhqk,bkhd->bqhd",
        weights.astype(jnp.bfloat16),
        values_all,
        preferred_element_type=jnp.float32,
    )
    attended = attended.reshape(tok_rows, local_width).astype(jnp.bfloat16)
    partial_out = jnp.dot(
        attended,
        lax.all_gather(w_out, "dp", axis=1, tiled=True),
        preferred_element_type=jnp.float32,
    )
    attention = lax.psum(partial_out, "mp")
    hidden_state = input_tokens + attention + bias_out.astype(jnp.float32)[None, :]
    second_standardized, second_inverse_deviation = apply_norm(hidden_state)
    second_normalized = (second_standardized * second_gain_f32[None, :]).astype(jnp.bfloat16)
    logits = jnp.dot(second_normalized, router_all, preferred_element_type=jnp.float32)
    gate_probs = jax.nn.softmax(logits, axis=-1)
    choose = (routes[:, :, None] == jnp.arange(experts, dtype=jnp.int32)[None, None, :]).astype(
        jnp.float32
    )
    gate_values = jnp.sum(choose * gate_probs[:, None, :], axis=2)
    slot_index = routing(routes, priority[0], experts, capacity)
    slot_pair = pair_of_slot(slot_index, experts, capacity)
    zero_row = jnp.zeros((1, D), jnp.bfloat16)
    padded_two = jnp.concatenate([second_normalized, zero_row], axis=0)
    outgoing = padded_two[slot_pair // 2].reshape(experts, capacity, D)
    received = to_experts(outgoing)
    pre_act = (
        jnp.dot(received, w_in[0], preferred_element_type=jnp.float32)
        + in_bias[0].astype(jnp.float32)[None, :]
    )
    act_values, gelu_back = jax.vjp(partial(jax.nn.gelu, approximate=False), pre_act)
    act_low = act_values.astype(jnp.bfloat16)
    partial_y = jnp.dot(act_low, w_back[0], preferred_element_type=jnp.float32)
    returned = from_experts(partial_y, back_bias[0].astype(jnp.float32))
    padded_back = jnp.concatenate([returned, zero_row], axis=0)
    picked = padded_back[slot_index].astype(jnp.float32)
    mixture = hidden_state + jnp.sum(gate_values[:, :, None] * picked, axis=1)
    output = mixture.astype(jnp.bfloat16)
    output_gradient = cotangent.astype(jnp.float32)
    grad_gates = jnp.sum(output_gradient[:, None, :] * picked, axis=2)
    pair_grads = (
        (gate_values[:, :, None] * output_gradient[:, None, :])
        .astype(jnp.bfloat16)
        .reshape(2 * tok_rows, D)
    )
    padded_pairs = jnp.concatenate([pair_grads, zero_row], axis=0)
    grad_send = padded_pairs[slot_pair].reshape(experts, capacity, D)
    grad_recv = to_experts(grad_send)
    grad_back_bias = jnp.sum(grad_recv, axis=0, dtype=jnp.float32)[None]
    grad_w_back = contract_first(act_low, grad_recv)[None]
    grad_act = contract_last(grad_recv, w_back[0])
    grad_pre = gelu_back(grad_act)[0].astype(jnp.bfloat16)
    grad_in_bias = jnp.sum(grad_pre, axis=0, dtype=jnp.float32)[None]
    grad_w_in = contract_first(received, grad_pre)[None]
    partial_x = contract_last(grad_pre, w_in[0])
    grad_rows = from_experts(partial_x, jnp.zeros((D,), jnp.float32))
    padded_grad = jnp.concatenate([grad_rows, zero_row], axis=0)
    second_norm_gradient = jnp.sum(padded_grad[slot_index].astype(jnp.float32), axis=1)
    grad_probs = jnp.sum(grad_gates[:, :, None] * choose, axis=1)
    grad_logits = gate_probs * (
        grad_probs - jnp.sum(grad_probs * gate_probs, axis=-1, keepdims=True)
    )
    logits_low = grad_logits.astype(jnp.bfloat16)
    grad_router = contract_first(second_normalized, logits_low)
    second_norm_gradient = second_norm_gradient + contract_last(logits_low, router_all)
    second_gain_gradient = jnp.sum(second_norm_gradient * second_standardized, axis=0)
    hidden_gradient = output_gradient + norm_backward(
        second_norm_gradient, second_gain_f32, second_standardized, second_inverse_deviation
    )
    grad_out_bias = jnp.sum(hidden_gradient, axis=0)
    grad_low = hidden_gradient.astype(jnp.bfloat16)
    grad_w_out = contract_first(attended, grad_low)
    column_total = grad_low
    grad_attended = contract_last(column_total, lax.all_gather(w_out, "dp", axis=1, tiled=True))
    grad_att_low = grad_attended.astype(jnp.bfloat16).reshape(images, SEQ, local_heads, HD)
    scores_again = (
        jnp.einsum("bqhd,bkhd->bhqk", queries, keys_all, preferred_element_type=jnp.float32)
        * score_scale
    )
    weights_again = jnp.exp(scores_again - log_total)
    grad_values = jnp.einsum(
        "bhqk,bqhd->bkhd",
        weights_again.astype(jnp.bfloat16),
        grad_att_low,
        preferred_element_type=jnp.float32,
    )
    grad_weights = jnp.einsum(
        "bqhd,bkhd->bhqk", grad_att_low, values_all, preferred_element_type=jnp.float32
    )
    grad_scores = weights_again * (
        grad_weights - jnp.sum(grad_weights * weights_again, axis=-1, keepdims=True)
    )
    scores_low = grad_scores.astype(jnp.bfloat16)
    grad_queries = (
        jnp.einsum("bhqk,bkhd->bqhd", scores_low, keys_all, preferred_element_type=jnp.float32)
        * score_scale
    )
    grad_keys = (
        jnp.einsum("bhqk,bqhd->bkhd", scores_low, queries, preferred_element_type=jnp.float32)
        * score_scale
    )
    grad_merged = (
        jnp.stack([grad_queries, grad_keys, grad_values], axis=2)
        .astype(jnp.bfloat16)
        .reshape(tok_rows, 3 * local_width)
    )
    grad_w_qkv = contract_first(first_normalized, grad_merged).reshape(D, 3, local_width)
    portion = lax.all_gather(w_qkv, "dp", axis=0, tiled=True)
    grad_part = contract_last(grad_merged, portion.reshape(portion.shape[0], -1))
    first_norm_gradient = lax.psum(grad_part.astype(jnp.bfloat16), "mp").astype(jnp.float32)
    first_gain_gradient = jnp.sum(first_norm_gradient * first_standardized, axis=0)
    token_gradient = (
        hidden_gradient
        + norm_backward(
            first_norm_gradient, first_gain_f32, first_standardized, first_inverse_deviation
        )
    ).astype(jnp.bfloat16)
    row_grads = (
        lax.psum_scatter(grad_w_qkv, "dp", scatter_dimension=0, tiled=True),
        lax.psum_scatter(first_gain_gradient, "dp", scatter_dimension=0, tiled=True),
        lax.psum_scatter(second_gain_gradient, "dp", scatter_dimension=0, tiled=True),
        lax.psum_scatter(grad_out_bias, "dp", scatter_dimension=0, tiled=True),
        lax.psum_scatter(grad_router, "dp", scatter_dimension=0, tiled=True),
    )
    grad_w_out_shard = lax.psum_scatter(grad_w_out, "dp", scatter_dimension=1, tiled=True)
    return (
        output,
        token_gradient,
        row_grads[1],
        row_grads[0],
        grad_w_out_shard,
        row_grads[3],
        row_grads[2],
        row_grads[4],
        grad_w_in,
        grad_in_bias,
        grad_w_back,
        grad_back_bias,
    )


def solution(mesh):
    return jax.shard_map(
        body,
        mesh=mesh,
        in_specs=(
            P("dp", None),
            P("dp"),
            P("dp", None, "mp"),
            P("mp", "dp"),
            P("dp"),
            P("dp"),
            P("dp", None),
            P("dp", None, "mp"),
            P("dp", "mp"),
            P("dp", "mp", None),
            P("dp", None),
            P("dp", None),
            P("dp", None),
            P("dp", None),
        ),
        out_specs=(
            P("dp", None),
            P("dp", None),
            P("dp"),
            P("dp", None, "mp"),
            P("mp", "dp"),
            P("dp"),
            P("dp"),
            P("dp", None),
            P("dp", None, "mp"),
            P("dp", "mp"),
            P("dp", "mp", None),
            P("dp", None),
        ),
        check_vma=False,
    )
```

profile of v0, /device:TPU:9, one launch (start us, length us, event | category | flops | bytes accessed | tf_op | source)
XLA Modules:
  0.0 1121.7 jit_solution(5199220580727626139)
XLA Ops:
  12.5 29.1 %all-reduce.12 = (bf16[768]{0:T(1024)(128)(2,1)S(1)}, bf16[768]{0:T(1024)(128)(2,1)S(1)}, bf16[768]{0:T(1024)(128)(2,1)S(1)}) all-reduce(bf16[768]{0:T(1024)(128)(2,1)S(1)} %dynamic-update-slice, bf16[768]{0:T(1024)(128)(2,1)S(1)} %dynamic-update-slice.1, bf16[768]{0:T(1024)(128)(2,1)S(1)} %dynamic-update-slice.2), channel_id=1, replica_groups=mesh['dp'=16,'mp'=2] {'dp'}, use_global_device_ids=true, to_apply=%add.5 | all-reduce | flops 2304 | bytes 9216
  49.9 37.1 %all_gather.34 = bf16[384,768]{0,1:T(8,128)(2,1)} all-gather(bf16[384,48]{0,1:T(8,128)(2,1)S(1)} %copy-done.49), channel_id=1, replica_groups=mesh['dp'=16,'mp'=2] {'dp'}, dimensions={1}, use_global_device_ids=true | all-gather | bytes 626688 | tf_op jit(solution)/shard_map/all_gather | solution.py:168
  155.7 11.5 %gather_fusion = s32[1970]{0:T(1024)S(1)} fusion(s32[1970]{0:T(1024)S(1)} %fusion.55, s32[2048]{0:T(1024)S(1)} %pad_clamp_fusion.3), kind=kCustom, calls=%fused_computation | custom fusion | bytes 23640 | tf_op jit(solution)/shard_map/gather | solution.py:25
  186.2 11.8 %gather_fusion.1 = bf16[2448,768]{1,0:T(8,128)(2,1)} fusion(bf16[986,768]{1,0:T(8,128)(2,1)} %concatenate.12, s32[3072]{0:T(1024)S(1)} %get-tuple-element.53), kind=kCustom, calls=%fused_computation.1 | custom fusion | bytes 7530048 | tf_op jit(solution)/shard_map/gather | solution.py:185
  205.1 10.4 all-to-all-start
  215.5 58.8 %all-gather = bf16[16,48,16]{1,2,0:T(8,128)(2,1)S(1)} all-gather(bf16[1,48,16]{1,2,0:T(8,128)(2,1)S(1)} %bitcast.127), channel_id=1, replica_groups=mesh['dp'=16,'mp'=2] {'dp'}, dimensions={0}, use_global_device_ids=true | all-gather | bytes 26112 | tf_op jit(solution)/shard_map/all_gather | solution.py:124
  297.2 12.5 %gather_fusion.3 = bf16[2448,768]{1,0:T(8,128)(2,1)} fusion(bf16[1971,768]{1,0:T(8,128)(2,1)} %concatenate.14, s32[3072]{0:T(1024)S(1)} %get-tuple-element.52), kind=kCustom, calls=%fused_computation.3 | custom fusion | bytes 7530048 | tf_op jit(solution)/shard_map/gather | solution.py:207
  322.9 40.7 %all-to-all-done.2 = bf16[16,153,384]{2,1,0:T(8,128)(2,1)} async-done(((bf16[16,153,384]{2,1,0:T(8,128)(2,1)}), bf16[16,153,384]{2,1,0:T(8,128)(2,1)}, u32[]{:S(2)}, u32[]{:S(2)}) %all-to-all-start.2) | async-done | bytes 1880096 | tf_op jit(solution)/shard_map/all_to_all | solution.py:69
  367.7 39.9 %multiply_convert_fusion = (bf16[2448,1536]{1,0:T(8,128)(2,1)}, f32[2448,1536]{1,0:T(8,128)}, f32[2448,1536]{1,0:T(8,128)}) fusion(f32[1536]{0:T(1024)S(1)} %convert_reduce_fusion.3, bf16[2448,768]{1,0:T(8,128)(2,1)} %reshape.284, bf16[1,768,1536]{2,1,0:T(8,128)(2,1)S(1)} %copy-done), kind=kOutput, calls=%fused_computation.11 | convolution fusion | flops 6023725056 | bytes 43726848 | tf_op jit(solution)/shard_map/dot_general | solution.py:188
  411.6 21.4 %convert_reduce_fusion = (f32[1536]{0:T(1024)S(1)}, bf16[2448,1536]{1,0:T(8,128)(2,1)}) fusion(f32[2448,1536]{1,0:T(8,128)} %get-tuple-element.31, bf16[2448,768]{1,0:T(8,128)(2,1)} %reshape.288, bf16[1,1536,768]{2,1,0:T(8,128)(2,1)} %param.23, f32[2448,1536]{1,0:T(8,128)} %get-tuple-element.44, f32[1536]{0:T(1024)S(1)} %convert_reduce_fusion.3), kind=kOutput, calls=%fused_computation.9 | convolution fusion | flops 5839477248 | bytes 43732992 | tf_op jit(solution)/shard_map/dot_general | solution.py:57
  433.0 10.5 fusion.32
  443.6 10.9 fusion.30
  477.3 43.5 %all-to-all-done.3 = bf16[16,153,384]{2,1,0:T(8,128)(2,1)} async-done(((bf16[16,153,384]{2,1,0:T(8,128)(2,1)}), bf16[16,153,384]{2,1,0:T(8,128)(2,1)}, u32[]{:S(2)}, u32[]{:S(2)}) %all-to-all-start.3) | async-done | bytes 1880096 | tf_op jit(solution)/shard_map/all_to_all | solution.py:69
  527.3 51.1 %all_to_all.20 = bf16[16,153,384]{2,1,0:T(8,128)(2,1)} all-to-all(bf16[16,153,384]{2,1,0:T(8,128)(2,1)} %reshape.285), channel_id=1, replica_groups=mesh['dp'=16,'mp'=2] {'dp'}, dimensions={0} | all-to-all | bytes 3760128 | tf_op jit(solution)/shard_map/all_to_all | solution.py:69
  591.2 12.6 %gather_fusion.4 = bf16[1970,768]{1,0:T(8,128)(2,1)} fusion(bf16[2449,768]{1,0:T(8,128)(2,1)} %concatenate.15, s32[2048]{0:T(1024)S(1)} %pad_clamp_fusion.2), kind=kCustom, calls=%fused_computation.4 | custom fusion | bytes 6059720 | tf_op jit(solution)/shard_map/gather | solution.py:218
  612.0 12.6 %gather_fusion.2 = bf16[1970,768]{1,0:T(8,128)(2,1)} fusion(bf16[2449,768]{1,0:T(8,128)(2,1)} %concatenate.13, s32[2048]{0:T(1024)S(1)} %pad_clamp_fusion.2), kind=kCustom, calls=%fused_computation.2 | custom fusion | bytes 6059720 | tf_op jit(solution)/shard_map/gather | solution.py:196
  632.3 16.8 %multiply_reduce_fusion.1 = (f32[985,2]{1,0:T(8,128)S(1)}, f32[985,768]{1,0:T(8,128)}) fusion(f32[985,2,768]{2,1,0:T(2,128)} %reshape.357, f32[985,768]{1,0:T(8,128)} %convert_element_type.136, f32[985,2]{1,0:T(8,128)S(1)} %copy-done.15), kind=kLoop, calls=%fused_computation.32 | loop fusion | flops 5293390 | bytes 12119440 | tf_op jit(solution)/shard_map/reduce_sum | solution.py:200
  659.9 11.5 %reduce_sum.216 = f32[985,768]{1,0:T(8,128)} reduce(f32[985,2,768]{2,1,0:T(2,128)} %reshape.358, f32[]{:T(128)} %constant.50.clone.1), dimensions={1}, to_apply=%region_18.19 | reduce | flops 756480 | bytes 9077764 | tf_op jit(solution)/shard_map/reduce_sum | solution.py:218
  738.9 10.4 convolution_bitcast_fusion.1
  759.5 63.3 %reduce-scatter.16.cloned.1.call-done = f32[48,16]{1,0:T(8,128)} async-done(((f32[768,16]{1,0:T(8,128)}), f32[48,16]{1,0:T(8,128)}) %reduce-scatter.16.cloned.1.call-update) | async-done | bytes 3088
  824.2 23.4 %all-reduce.18.cloned.1.call-done = bf16[985,768]{1,0:T(8,128)(2,1)} async-done(((bf16[985,768]{1,0:T(8,128)(2,1)}), bf16[985,768]{1,0:T(8,128)(2,1)}) %all-reduce.18.cloned.1.call-update) | async-done | bytes 1512976 | tf_op jit(solution)/shard_map/psum | solution.py:270
  851.0 57.2 %all-reduce.11 = (f32[768]{0:T(1024)S(1)}, f32[768]{0:T(1024)S(1)}, f32[768]{0:T(1024)S(1)}) all-reduce(f32[768]{0:T(1024)S(1)} %get-tuple-element.16, f32[768]{0:T(1024)S(1)} %get-tuple-element.26, f32[768]{0:T(1024)S(1)} %get-tuple-element.12), channel_id=4, replica_groups=mesh['dp'=16,'mp'=2] {'dp'}, use_global_device_ids=true, to_apply=%region_29.30.clone | all-reduce | flops 2304 | bytes 18432
  914.2 61.8 %reduce-scatter.14.cloned.1.call-done = f32[384,48]{0,1:T(8,128)} async-done(((f32[384,768]{0,1:T(8,128)}), f32[384,48]{0,1:T(8,128)}) %reduce-scatter.14.cloned.1.call-update) | async-done | bytes 73744 | tf_op jit(solution)/shard_map/reduce_scatter | solution.py:285
  976.0 138.7 %reduce-scatter.12.cloned.1.call-done = f32[48,3,384]{2,0,1:T(8,128)} async-done(((f32[768,3,384]{2,0,1:T(8,128)}), f32[48,3,384]{2,0,1:T(8,128)}) %reduce-scatter.12.cloned.1.call-update) | async-done | bytes 221200 | tf_op jit(solution)/shard_map/reduce_scatter | solution.py:279
  (281 shorter events, 307.4 us)
Async XLA Ops:
  7.2 360.6 %copy-start = (bf16[1,768,1536]{2,1,0:T(8,128)(2,1)S(1)}, bf16[1,768,1536]{2,1,0:T(8,128)(2,1)}, u32[]{:S(2)}) copy-start(bf16[1,768,1536]{2,1,0:T(8,128)(2,1)} %param.21) | copy-start | bytes 7077892
  7.2 42.7 %copy-start.49 = (bf16[384,48]{0,1:T(8,128)(2,1)S(1)}, bf16[384,48]{0,1:T(8,128)(2,1)}, u32[]{:S(2)}) copy-start(bf16[384,48]{0,1:T(8,128)(2,1)} %param.17) | copy-start | bytes 110596
  7.2 79.8 %all-gather.7.cloned.1.call-start = ((), (), s32[]{:S(2)}) async-start(), calls=%async_computation.9 | async-start | bytes 1880064 | tf_op jit(solution)/shard_map/all_gather | solution.py:120
  7.9 172.2 %all-reduce.16.cloned.1.call-start = ((), (), s32[]{:S(2)}) async-start(), calls=%async_computation.10 | async-start | bytes 6094848 | tf_op jit(solution)/shard_map/psum | solution.py:171
  41.6 49.3 %copy-start.45 = (f32[768]{0:T(1024)}, f32[768]{0:T(1024)S(1)}, u32[]{:S(2)}) copy-start(f32[768]{0:T(1024)S(1)} %convert_element_type.120) | copy-start | bytes 9220
  47.9 48.6 %copy-start.37 = (f32[985]{0:T(1024)}, f32[985]{0:T(1024)S(1)}, u32[]{:S(2)}) copy-start(f32[985]{0:T(1024)S(1)} %broadcast_multiply_fusion.6) | copy-start | bytes 11824
  49.9 46.6 %copy-start.47 = (f32[985]{0:T(1024)}, f32[985]{0:T(1024)S(1)}, u32[]{:S(2)}) copy-start(f32[985]{0:T(1024)S(1)} %add_rsqrt_fusion.1) | copy-start | bytes 11824
  155.7 24.4 %copy-start.51 = (f32[768]{0:T(1024)S(1)}, f32[768]{0:T(1024)}, u32[]{:S(2)}) copy-start(f32[768]{0:T(1024)} %convert_element_type.127) | copy-start | bytes 9220
  205.1 87.2 %all-to-all-start = ((bf16[16,153,384]{2,1,0:T(8,128)(2,1)}), bf16[16,153,384]{2,1,0:T(8,128)(2,1)}, u32[]{:S(2)}, u32[]{:S(2)}) async-start(bf16[16,153,384]{2,1,0:T(8,128)(2,1)} %constant_dynamic-slice_fusion.1), calls=%async_computation | async-start | bytes 3932160 | tf_op jit(solution)/shard_map/all_to_all | solution.py:69
  215.5 148.3 %all-gather.9.cloned.1.call-start = ((), (), s32[]{:S(2)}) async-start(), calls=%async_computation.11 | async-start | bytes 5898240 | tf_op jit(solution)/shard_map/all_gather | solution.py:73
  317.2 46.4 %all-to-all-start.2 = ((bf16[16,153,384]{2,1,0:T(8,128)(2,1)}), bf16[16,153,384]{2,1,0:T(8,128)(2,1)}, u32[]{:S(2)}, u32[]{:S(2)}) async-start(bf16[16,153,384]{2,1,0:T(8,128)(2,1)} %constant_dynamic-slice_fusion), calls=%async_computation.3 | async-start | bytes 3932160 | tf_op jit(solution)/shard_map/all_to_all | solution.py:69
  322.8 84.8 %all-gather.13.cloned.1.call-start = ((), (), s32[]{:S(2)}) async-start(), calls=%async_computation.14 | async-start | bytes 5898240 | tf_op jit(solution)/shard_map/all_gather | solution.py:73
  363.7 100.9 %reduce-scatter.10.cloned.1.call-start = ((), (), s32[]{:S(2)}) async-start(), calls=%async_computation.15 | async-start | bytes 11280384 | tf_op jit(solution)/shard_map/reduce_scatter | solution.py:85
  443.5 77.4 %reduce-scatter.8.cloned.1.call-start = ((), (), s32[]{:S(2)}) async-start(), calls=%async_computation.12 | async-start | bytes 11280384 | tf_op jit(solution)/shard_map/reduce_scatter | solution.py:85
  470.8 50.0 %all-to-all-start.3 = ((bf16[16,153,384]{2,1,0:T(8,128)(2,1)}), bf16[16,153,384]{2,1,0:T(8,128)(2,1)}, u32[]{:S(2)}, u32[]{:S(2)}) async-start(bf16[16,153,384]{2,1,0:T(8,128)(2,1)} %reshape.289), calls=%async_computation.5 | async-start | bytes 3932160 | tf_op jit(solution)/shard_map/all_to_all | solution.py:69
  477.3 104.8 %all-gather.15.cloned.1.call-start = ((), (), s32[]{:S(2)}) async-start(), calls=%async_computation.16 | async-start | bytes 5898240 | tf_op jit(solution)/shard_map/all_gather | solution.py:73
  520.8 83.0 %all-gather.11.cloned.1.call-start = ((), (), s32[]{:S(2)}) async-start(), calls=%async_computation.13 | async-start | bytes 5898240 | tf_op jit(solution)/shard_map/all_gather | solution.py:73
  578.4 244.4 %reduce-scatter.16.cloned.1.call-start = ((), (), s32[]{:S(2)}) async-start(), calls=%async_computation.20 | async-start | bytes 417792
  632.2 17.1 %copy-start.24 = (f32[985,16]{0,1:T(8,128)S(1)}, f32[985,16]{0,1:T(8,128)}, u32[]{:S(2)}) copy-start(f32[985,16]{0,1:T(8,128)} %copy-done.23) | copy-start | bytes 189124
  632.2 17.1 %copy-start.34 = (f32[985]{0:T(1024)S(1)}, f32[985]{0:T(1024)}, u32[]{:S(2)}) copy-start(f32[985]{0:T(1024)} %copy-done.33) | copy-start | bytes 11824
  632.2 17.1 %copy-start.40 = (f32[985]{0:T(1024)S(1)}, f32[985]{0:T(1024)}, u32[]{:S(2)}) copy-start(f32[985]{0:T(1024)} %copy-done.39) | copy-start | bytes 11824
  702.9 144.7 %all-reduce.18.cloned.1.call-start = ((), (), s32[]{:S(2)}) async-start(), calls=%async_computation.17 | async-start | bytes 3047424 | tf_op jit(solution)/shard_map/psum | solution.py:270
  723.4 252.7 %reduce-scatter.14.cloned.1.call-start = ((), (), s32[]{:S(2)}) async-start(), calls=%async_computation.19 | async-start | bytes 1253376 | tf_op jit(solution)/shard_map/reduce_scatter | solution.py:285
  727.4 387.3 %reduce-scatter.12.cloned.1.call-start = ((), (), s32[]{:S(2)}) async-start(), calls=%async_computation.18 | async-start | bytes 3760128 | tf_op jit(solution)/shard_map/reduce_scatter | solution.py:279
  (48 other events, 269.2 us)
Sparse Core Ops, SparseCore 0:
  10.7 61.1 all-gather.6
  136.3 39.8 all-reduce.15
  292.4 24.1 all-gather.8
  363.8 17.9 all-gather.12
  443.7 20.8 reduce-scatter.9
  466.7 17.2 reduce-scatter.7
  521.0 15.3 all-gather.14
  578.5 13.7 all-gather.10
  703.1 119.7 reduce-scatter.15
  825.7 21.8 all-reduce.17
  853.7 122.2 reduce-scatter.13
  982.3 132.3 reduce-scatter.11
where the time goes:
time: 1140 us; the launch traced here: 1120 us
  waiting for transfers between devices  382 us (34%)
  local copies, waits for them, and re-layouts  233 us (20%)
  blocking collectives  233 us (20%)
  matrix products  156 us (14%)
  other arithmetic  76.8 us (7%)
  starting transfers between devices  22.9 us (2%)
  between operations  16.7 us (1%)
    reduce_scatter x1, waiting for transfers between devices, body(): lax.psum_scatter(grad_w_qkv, 'dp', scatter_dimension=0, tiled=True)  139 us
    unnamed x2, blocking collectives  86.3 us
    all_to_all x3, waiting for transfers between devices, across_half(): return lax.all_to_all(values, 'dp', split_axis=0, concat_axis=0, tiled=True)  84.2 us
    unnamed x13, waiting for transfers between devices  64.2 us
    reduce_scatter x1, waiting for transfers between devices, body(): lax.psum_scatter(grad_w_out, 'dp', scatter_dimension=1, tiled=True)  61.8 us
    all_gather x1, blocking collectives, body(): part_router = lax.all_gather(router, 'dp', axis=0, tiled=True)  58.8 us
    all_to_all x1, blocking collectives, across_half(): return lax.all_to_all(values, 'dp', split_axis=0, concat_axis=0, tiled=True)  51.1 us
    dot_general x5, matrix products, contract_last(): lax.dot_general(left, right, (((1,), (1,)), ((), ())), preferred_element_...  42.7 us
  transfers between devices with their start and end apart: 15, of which 7 were waited for; matrix products, arithmetic and copies ran while one was open for 23% of the time, Pallas kernels for 0%

commit v1 on v0

v1 whole, which is shorter than its diff:
```python
import functools

import jax
import jax.numpy as jnp
from jax import lax
from jax.experimental import pallas as pl
from jax.experimental.pallas import tpu as pltpu
from jax.sharding import PartitionSpec as P

D = 768
HD = 64
SEQ = 197
EPS = 1e-06
F32 = jnp.float32
BF = jnp.bfloat16
MESH = pl.DeviceIdType.MESH
VMEM_LIMIT = 62 * 1024 * 1024
LINE = 4
FREE = 3


def up(value, step):
    return (value + step - 1) // step * step


SEQ_PAD = up(SEQ, 16)


def mm(left, right, cl, cr):
    return lax.dot_general(
        left, right, (((cl,), (cr,)), ((), ())), preferred_element_type=F32
    )


def norm_rows(values):
    average = jnp.mean(values, axis=-1, keepdims=True)
    centered = values - average
    inverse = lax.rsqrt(jnp.mean(centered * centered, axis=-1, keepdims=True) + EPS)
    return centered * inverse, inverse


def norm_back(grad, gain, xhat, inverse):
    scaled = grad * gain
    return inverse * (
        scaled
        - jnp.mean(scaled, axis=-1, keepdims=True)
        - xhat * jnp.mean(scaled * xhat, axis=-1, keepdims=True)
    )


def split_two(value):
    high = value.astype(BF)
    return high, (value - high.astype(F32)).astype(BF)


def whole():
    return pl.BlockSpec(memory_space=pltpu.VMEM)


def params(**more):
    return pltpu.CompilerParams(vmem_limit_bytes=VMEM_LIMIT, **more)


def greet(peers):
    barrier = pltpu.get_barrier_semaphore()
    for peer in peers:
        pl.semaphore_signal(barrier, inc=1, device_id=peer, device_id_type=MESH)
    pl.semaphore_wait(barrier, len(peers))


def remote(src, dst, send_sem, recv_sem, peer):
    return pltpu.make_async_remote_copy(
        src_ref=src, dst_ref=dst, send_sem=send_sem, recv_sem=recv_sem,
        device_id=peer, device_id_type=MESH,
    )


def slot_matrix(idx_ref, first, rows):
    number = lax.broadcasted_iota(jnp.int32, (rows, idx_ref.shape[1]), 0) + first
    hit = (number == idx_ref[0:1, :]) | (number == idx_ref[1:2, :])
    return jnp.where(hit, 1.0, 0.0).astype(BF)


def route_kernel(experts, cap, half, slots, prow_ref, pcol_ref, rt_ref, ct_ref, idx_ref, out_ref, ctp):
    lanes = rt_ref.shape[1]
    tok = ct_ref.shape[0]
    mine = lax.axis_index("mp")
    ctp[...] = jnp.zeros_like(ctp)
    ctp[0:tok, :] = ct_ref[...]
    number = lax.broadcasted_iota(jnp.int32, (experts, lanes), 0)
    hot = [jnp.where(number == rt_ref[j : j + 1, :], 1.0, 0.0) for j in range(2)]
    before = jnp.where(pcol_ref[...] < prow_ref[...], 1.0, 0.0).astype(BF)
    counts = [mm(h.astype(BF), before, 1, 0) for h in hot]
    counts[1] = counts[1] + jnp.sum(hot[0], axis=1, keepdims=True)
    for j in range(2):
        slot = jnp.sum(counts[j] * hot[j], axis=0, keepdims=True).astype(jnp.int32)
        place = slot - mine * half
        expert = rt_ref[j : j + 1, :]
        kept = (slot < cap) & (place >= 0) & (place < half) & (expert >= 0)
        idx_ref[j : j + 1, :] = jnp.where(kept, expert * slots + place, -1)

    group = 4 * slots

    def step(b, carry):
        rows = slot_matrix(idx_ref, b * group, group)
        block = mm(rows, ctp[...], 1, 0).astype(BF)
        out_ref[pl.ds(b * 4, 4)] = block.reshape(4, slots, D)
        return carry

    lax.fori_loop(0, experts // 4, step, 0)


def route(prow, pcol, rt, ct, experts, cap, half, slots):
    lanes = rt.shape[1]
    return pl.pallas_call(
        functools.partial(route_kernel, experts, cap, half, slots),
        out_shape=(
            jax.ShapeDtypeStruct((2, lanes), jnp.int32),
            jax.ShapeDtypeStruct((experts, slots, D), BF),
        ),
        in_specs=[whole()] * 4,
        out_specs=(whole(), whole()),
        scratch_shapes=[pltpu.VMEM((lanes, D), BF)],
        compiler_params=params(),
        name="route",
    )(prow, pcol, rt, ct)


def gather_kernel(n, w_ref, s_ref, wo_ref, so_ref, lsem, zs, zr, ps, pr):
    me = lax.axis_index("dp")
    plane = n // LINE
    z, q = me // plane, me % plane
    rp = w_ref.shape[1]
    zpeer = [((z + d) % LINE) * plane + q for d in range(1, LINE)]
    qpeer = [z * plane + (q + d) % plane for d in range(1, plane)]
    greet([{"dp": p} for p in zpeer + qpeer])

    def at(block):
        rows = pl.ds(pl.multiple_of(block * rp, rp), rp)
        return wo_ref.at[:, rows, :], so_ref.at[rows, :]

    own = at(me)
    local = [pltpu.make_async_copy(a, b, lsem.at[i]) for i, (a, b) in enumerate(zip((w_ref, s_ref), own))]
    for c in local:
        c.start()
    sends = []
    for d, p in enumerate(zpeer):
        for i, (a, b) in enumerate(zip((w_ref, s_ref), own)):
            c = remote(a, b, zs.at[d, i], zr.at[d, i], {"dp": p})
            c.start()
            sends.append(c)
    for d, p in enumerate(qpeer):
        for i, (a, b) in enumerate(zip((w_ref, s_ref), own)):
            c = remote(a, b, ps.at[d, 0, i], pr.at[d, 0, i], {"dp": p})
            c.start()
            sends.append(c)
    for k in range(1, LINE):
        block = at(((z + LINE - k) % LINE) * plane + q)
        for i in range(2):
            remote(block[i], block[i], zs.at[k - 1, i], zr.at[k - 1, i], {"dp": zpeer[0]}).wait_recv()
        for d, p in enumerate(qpeer):
            for i in range(2):
                c = remote(block[i], block[i], ps.at[d, k, i], pr.at[d, k, i], {"dp": p})
                c.start()
                sends.append(c)
    for d in range(1, plane):
        for k in range(LINE):
            block = at(((z + LINE - k) % LINE) * plane + (q + plane - d) % plane)
            for i in range(2):
                remote(block[i], block[i], ps.at[d - 1, k, i], pr.at[d - 1, k, i], {"dp": qpeer[0]}).wait_recv()
    for c in sends:
        c.wait_send()
    for c in local:
        c.wait()


def gather_weights(w, s, n):
    parts, rp, width = w.shape
    plane = n // LINE
    sem = pltpu.SemaphoreType.DMA
    return pl.pallas_call(
        functools.partial(gather_kernel, n),
        out_shape=(
            jax.ShapeDtypeStruct((parts, n * rp, width), BF),
            jax.ShapeDtypeStruct((n * rp, s.shape[1]), BF),
        ),
        in_specs=[whole()] * 2,
        out_specs=(whole(), whole()),
        scratch_shapes=[
            sem((2,)), sem((LINE - 1, 2)), sem((LINE - 1, 2)),
            sem((plane - 1, LINE, 2)), sem((plane - 1, LINE, 2)),
        ],
        compiler_params=params(collective_id=0, has_side_effects=True),
        name="gather_weights",
    )(w, s)


def attend_kernel(experts, tok_ref, small_ref, w_ref, qkv_ref, att_ref, part_ref, xp, pp):
    images = xp.shape[0]
    scale = HD ** (-0.5)
    gains = jnp.transpose(small_ref[...].astype(F32))
    gain = gains[experts : experts + 1, :]
    xp[:, SEQ_PAD - 16 : SEQ_PAD, :] = jnp.zeros((images, 16, D), F32)
    for i in range(images):
        xp[i, 0:SEQ, :] = tok_ref[i * SEQ : (i + 1) * SEQ, :].astype(F32)
    lane = lax.broadcasted_iota(jnp.int32, (1, 2 * HD), 1)
    masks = [jnp.where(lane // HD == h, 1.0, 0.0).astype(BF) for h in range(2)]
    valid = lax.broadcasted_iota(jnp.int32, (1, SEQ_PAD), 1) < SEQ

    def image(i, carry):
        xhat, _ = norm_rows(xp[i])
        normed = (xhat * gain).astype(BF)
        for c in range(3):
            qkv_ref[c, i] = mm(normed, w_ref[c], 1, 0).astype(BF)
        for p in range(w_ref.shape[2] // (2 * HD)):
            cols = slice(p * 2 * HD, (p + 1) * 2 * HD)
            q, k, v = (qkv_ref[c, i, :, cols] for c in range(3))
            outs = []
            for h in range(2):
                scores = mm(q * masks[h], k, 1, 1) * scale
                scores = jnp.where(valid, scores, -1e30)
                raised = jnp.exp(scores - jnp.max(scores, axis=-1, keepdims=True))
                weights = raised / jnp.sum(raised, axis=-1, keepdims=True)
                outs.append(mm(weights.astype(BF), v, 1, 0))
            att_ref[i, :, cols] = jnp.where(lane < HD, outs[0], outs[1]).astype(BF)
        pp[i] = mm(att_ref[i], w_ref[3], 1, 1)
        return carry

    lax.fori_loop(0, images, image, 0)
    for i in range(images):
        part_ref[i * SEQ : (i + 1) * SEQ, :] = pp[i, 0:SEQ, :]


def attend(tok, small, w, experts):
    images = tok.shape[0] // SEQ
    width = w.shape[2]
    return pl.pallas_call(
        functools.partial(attend_kernel, experts),
        out_shape=(
            jax.ShapeDtypeStruct((3, images, SEQ_PAD, width), BF),
            jax.ShapeDtypeStruct((images, SEQ_PAD, width), BF),
            jax.ShapeDtypeStruct(tok.shape, F32),
        ),
        in_specs=[whole()] * 3,
        out_specs=(whole(),) * 3,
        scratch_shapes=[
            pltpu.VMEM((images, SEQ_PAD, D), F32),
            pltpu.VMEM((images, SEQ_PAD, D), F32),
        ],
        compiler_params=params(),
        name="attend",
    )(tok, small, w)


def row_chunks(rows):
    return [(s, min(256, rows - s)) for s in range(0, rows, 256)]


def dispatch_kernel(
    n, half, part_ref, tok_ref, small_ref, idx_ref, hid_ref, n2_ref, prob_ref, x_ref,
    own, other, send, p2, hs, hr, ss, rs,
):
    me, mine = lax.axis_index("dp"), lax.axis_index("mp")
    tok = tok_ref.shape[0]
    slots = send.shape[1]
    experts = prob_ref.shape[0]
    sibling = {"mp": 1 - mine}
    greet([sibling] + [{"dp": (me + d) % n} for d in range(1, n)])
    own[own.shape[0] - 16 :, :] = jnp.zeros((16, D), BF)
    copies = []
    for c, (start, size) in enumerate(row_chunks(own.shape[0])):
        stop = min(start + size, tok)
        own[start:stop, :] = part_ref[start:stop, :].astype(BF)
        rows = pl.ds(start, size)
        copy = remote(own.at[rows, :], other.at[rows, :], hs.at[c], hr.at[c], sibling)
        copy.start()
        copies.append(copy)
    gains = jnp.transpose(small_ref[...].astype(F32))
    gain = gains[experts + 1 : experts + 2, :]
    bias = gains[experts + 2 : experts + 3, :]
    n2_ref[n2_ref.shape[0] - 64 :, :] = jnp.zeros((64, D), BF)
    for c, (start, size) in enumerate(row_chunks(own.shape[0])):
        stop = min(start + size, tok)
        copies[c].wait_recv()
        both = own[start:stop, :].astype(F32) + other[start:stop, :].astype(F32)
        hidden = tok_ref[start:stop, :].astype(F32) + both + bias
        hid_ref[start:stop, :] = hidden
        xhat, _ = norm_rows(hidden)
        n2_ref[start:stop, :] = (xhat * gain).astype(BF)
    logits = mm(gains[0:experts, :].astype(BF), n2_ref[...], 1, 1)
    raised = jnp.exp(logits - jnp.max(logits, axis=0, keepdims=True))
    probs = raised / jnp.sum(raised, axis=0, keepdims=True)
    prob_ref[...] = probs
    high, low = split_two(probs)
    p2[0:experts, :] = high
    p2[experts:, :] = low
    place = lax.broadcasted_iota(jnp.int32, (slots, slots), 0)
    number = lax.broadcasted_iota(jnp.int32, (2 * experts, slots), 0)

    def step(b, carry):
        hot = [slot_matrix(idx_ref, ((me + b * 4 + j) % n) * slots, slots) for j in range(4)]
        block = mm(jnp.concatenate(hot, axis=0), n2_ref[...], 1, 0)
        for j in range(4):
            d = b * 4 + j
            peer = (me + d) % n
            gates = mm(p2[...], hot[j], 1, 1)
            row_high = jnp.sum(jnp.where(number == peer, gates, 0.0), axis=0, keepdims=True)
            row_low = jnp.sum(jnp.where(number == peer + experts, gates, 0.0), axis=0, keepdims=True)
            rows = block[j * slots : (j + 1) * slots, :]
            left = jnp.where(place == half, row_high, jnp.where(place == half + 1, row_low, rows[:, 0:slots]))
            send[d, :, :] = rows.astype(BF)
            send[d, :, 0:slots] = left.astype(BF)

            @pl.when(d > 0)
            def _():
                remote(send.at[d], x_ref.at[me], ss.at[d], rs.at[d], {"dp": peer}).start()

        return carry

    lax.fori_loop(0, n // 4, step, 0)
    x_ref[me] = send[0]

    def finish(d, carry):
        source = (me + n - d) % n
        remote(send.at[d], x_ref.at[source], ss.at[d], rs.at[d], {"dp": source}).wait()
        return carry

    lax.fori_loop(1, n, finish, 0)
    for copy in copies:
        copy.wait_send()


def dispatch(part, tok, small, idx, n, experts, half, slots):
    lanes = idx.shape[1]
    tr = up(tok.shape[0], 16)
    sem = pltpu.SemaphoreType.DMA
    chunks = len(row_chunks(tr))
    return pl.pallas_call(
        functools.partial(dispatch_kernel, n, half),
        out_shape=(
            jax.ShapeDtypeStruct(tok.shape, F32),
            jax.ShapeDtypeStruct((lanes, D), BF),
            jax.ShapeDtypeStruct((experts, lanes), F32),
            jax.ShapeDtypeStruct((n, slots, D), BF),
        ),
        in_specs=[whole()] * 4,
        out_specs=(whole(),) * 4,
        scratch_shapes=[
            pltpu.VMEM((tr, D), BF),
            pltpu.VMEM((tr, D), BF),
            pltpu.VMEM((n, slots, D), BF),
            pltpu.VMEM((2 * experts, lanes), BF),
            sem((chunks,)), sem((chunks,)), sem((n,)), sem((n,)),
        ],
        compiler_params=params(collective_id=1, has_side_effects=True),
        name="dispatch",
    )(part, tok, small, idx)


def expert_kernel(
    n, half, slots,
    x_ref, ct_ref, wi_own, wi_sib, wb_own, wb_sib, bi_own, bi_sib, bb_ref,
    gi_own, gi_sib, gb_own, gb_sib, gbi_own, gbi_sib, gbb_ref, dx_ref, y_ref,
    xt, g_s, y_acc, dx_acc, act_s, dpre_s, gate_s, wi_s, wb_s,
):
    k, steps = pl.program_id(0), pl.num_programs(0)
    first = k < steps // 2
    rows_all = n * slots
    tile = 256
    tiles = rows_all // tile

    def in_group():
        row = lax.broadcasted_iota(jnp.int32, (tile, n), 0)
        return row, lax.broadcasted_iota(jnp.int32, (tile, n), 1)

    @pl.when(k == 0)
    def _():
        group = lax.broadcasted_iota(jnp.int32, (n, rows_all), 0)
        row = lax.broadcasted_iota(jnp.int32, (n, rows_all), 1)
        pick = jnp.where((row == group * slots + half) | (row == group * slots + half + 1), 1.0, 0.0)
        gates = mm(pick.astype(BF), x_ref[:, 0:128], 1, 0)
        high, low = split_two(gates)

        def start(r, total):
            at = pl.ds(pl.multiple_of(r * tile, tile), tile)
            row, group = in_group()
            mine = jnp.where((row + r * tile) // slots == group, 1.0, 0.0).astype(BF)
            wide = mm(mine, high, 1, 0) + mm(mine, low, 1, 0)
            spot = lax.broadcasted_iota(jnp.int32, (tile, 128), 0) + r * tile
            lane = lax.broadcasted_iota(jnp.int32, (tile, 128), 1)
            gate = jnp.sum(jnp.where(lane == spot % slots, wide, 0.0), axis=1, keepdims=True)
            gate_s[at, :] = gate
            scaled = (gate * ct_ref[at, :].astype(F32)).astype(BF)
            g_s[at, :] = scaled
            xt[:, at] = jnp.transpose(x_ref[at, :].astype(F32)).astype(BF)
            return total + jnp.sum(scaled.astype(F32), axis=0, keepdims=True)

        gbb_ref[...] = lax.fori_loop(0, tiles, start, jnp.zeros((1, D), F32))
        y_acc[...] = jnp.zeros_like(y_acc)
        dx_acc[...] = jnp.zeros_like(dx_acc)

    @pl.when(first)
    def _():
        wi_s[...] = wi_own[...]
        wb_s[...] = wb_own[...]

    @pl.when(jnp.logical_not(first))
    def _():
        wi_s[...] = wi_sib[...]
        wb_s[...] = wb_sib[...]

    bias = jnp.where(first, bi_own[...], bi_sib[...]).astype(F32)

    def forward(r, total):
        at = pl.ds(pl.multiple_of(r * tile, tile), tile)
        pre = mm(x_ref[at, :], wi_s[...], 1, 0) + bias
        phi = 0.5 * (1.0 + lax.erf(pre * (0.5**0.5)))
        slope = phi + pre * (jnp.exp(-0.5 * pre * pre) * ((2.0 * jnp.pi) ** -0.5))
        act = (pre * phi).astype(BF)
        act_s[at, :] = act
        grad = (mm(g_s[at, :], wb_s[...], 1, 1) * slope).astype(BF)
        dpre_s[at, :] = grad
        y_acc[at, :] += mm(act, wb_s[...], 1, 0)
        dx_acc[at, :] += mm(grad, wi_s[...], 1, 1)
        return total + jnp.sum(grad.astype(F32), axis=0, keepdims=True)

    total = lax.fori_loop(0, tiles, forward, jnp.zeros(bias.shape, F32))

    def first_weight(r, carry):
        at = pl.ds(pl.multiple_of(r * tile, tile), tile)
        grad = mm(xt[at, :], dpre_s[...], 1, 0)

        @pl.when(first)
        def _():
            gi_own[at, :] = grad

        @pl.when(jnp.logical_not(first))
        def _():
            gi_sib[at, :] = grad.astype(BF)

        return carry

    lax.fori_loop(0, D // tile, first_weight, 0)

    def second_weight(r, carry):
        at = pl.ds(pl.multiple_of(r * tile, tile), tile)
        grad = mm(act_s[:, at], g_s[...], 0, 0)

        @pl.when(first)
        def _():
            gb_own[at, :] = grad

        @pl.when(jnp.logical_not(first))
        def _():
            gb_sib[at, :] = grad.astype(BF)

        return carry

    lax.fori_loop(0, act_s.shape[1] // tile, second_weight, 0)

    @pl.when(first)
    def _():
        gbi_own[...] = total

    @pl.when(jnp.logical_not(first))
    def _():
        gbi_sib[...] = total

    @pl.when(k == steps - 1)
    def _():
        def finish(r, sums):
            at = pl.ds(pl.multiple_of(r * tile, tile), tile)
            y = (y_acc[at, :] + bb_ref[...].astype(F32)).astype(BF).astype(F32)
            y_ref[at, :] = (gate_s[at, :] * y).astype(BF)
            dots = jnp.sum(ct_ref[at, :].astype(F32) * y, axis=1, keepdims=True)
            spot = lax.broadcasted_iota(jnp.int32, (tile, 128), 0) + r * tile
            lane = lax.broadcasted_iota(jnp.int32, (tile, 128), 1)
            spread = jnp.where(lane == spot % slots, dots, 0.0)
            row, group = in_group()
            mine = jnp.where((row + r * tile) // slots == group, 1.0, 0.0).astype(BF)
            high, low = split_two(spread)
            return sums[0] + mm(mine, high, 0, 0), sums[1] + mm(mine, low, 0, 0)

        zero = jnp.zeros((n, 128), F32)
        high, low = lax.fori_loop(0, tiles, finish, (zero, zero))
        high, low = high.astype(BF), low.astype(BF)

        def leave(r, carry):
            at = pl.ds(pl.multiple_of(r * tile, tile), tile)
            row, group = in_group()
            spot = row + r * tile - group * slots
            put = [jnp.where(spot == half + i, 1.0, 0.0).astype(BF) for i in range(2)]
            dx_ref[at, :] = dx_acc[at, :].astype(BF)
            dx_ref[at, 0:128] = (dx_acc[at, 0:128] + mm(put[0], high, 1, 0) + mm(put[1], low, 1, 0)).astype(BF)
            return carry

        lax.fori_loop(0, tiles, leave, 0)


def expert(x, ct, wi, wb, bi, bb, n, half, slots):
    rows = n * slots
    hidden = wi[0].shape[1]
    chunk = 512
    each = hidden // chunk
    own = lambda k: jnp.minimum(k, each - 1)
    sib = lambda k: jnp.maximum(k - each, 0)
    cols = lambda at: pl.BlockSpec((D, chunk), lambda k: (0, at(k)))
    lines = lambda at: pl.BlockSpec((chunk, D), lambda k: (at(k), 0))
    strip = lambda at: pl.BlockSpec((1, chunk), lambda k: (0, at(k)))
    shape = jax.ShapeDtypeStruct
    return pl.pallas_call(
        functools.partial(expert_kernel, n, half, slots),
        grid=(2 * each,),
        out_shape=(
            shape((D, hidden), F32), shape((D, hidden), BF),
            shape((hidden, D), F32), shape((hidden, D), BF),
            shape((1, hidden), F32), shape((1, hidden), F32), shape((1, D), F32),
            shape((rows, D), BF), shape((rows, D), BF),
        ),
        in_specs=[whole(), whole(), cols(own), cols(sib), lines(own), lines(sib), strip(own), strip(sib), whole()],
        out_specs=(
            cols(own), cols(sib), lines(own), lines(sib), strip(own), strip(sib), whole(), whole(), whole(),
        ),
        scratch_shapes=[
            pltpu.VMEM((D, rows), BF),
            pltpu.VMEM((rows, D), BF),
            pltpu.VMEM((rows, D), F32),
            pltpu.VMEM((rows, D), F32),
            pltpu.VMEM((rows, chunk), BF),
            pltpu.VMEM((rows, chunk), BF),
            pltpu.VMEM((rows, 1), F32),
            pltpu.VMEM((D, chunk), BF),
            pltpu.VMEM((chunk, D), BF),
        ],
        compiler_params=params(dimension_semantics=("arbitrary",)),
        name="expert",
    )(x, ct, wi[0], wi[1], wb[0], wb[1], bi[0], bi[1], bb)


def return_kernel(
    n, half, dx_ref, idx_ref, prob_ref, n2_ref, hid_ref, ct_ref, small_ref, hg_ref, sg_ref,
    back, acc, own, other, gp, gp_other, ss, rs, hs, hr,
):
    me, mine = lax.axis_index("dp"), lax.axis_index("mp")
    tok = ct_ref.shape[0]
    slots = dx_ref.shape[1]
    experts = prob_ref.shape[0]
    sibling = {"mp": 1 - mine}
    greet([sibling] + [{"dp": (me + d) % n} for d in range(1, n)])

    def begin(d, carry):
        peer = (me + d) % n
        remote(dx_ref.at[peer], back.at[d], ss.at[d], rs.at[d], {"dp": peer}).start()
        return carry

    lax.fori_loop(1, n, begin, 0)
    back[0] = dx_ref[me]
    acc[...] = jnp.zeros_like(acc)
    gp[...] = jnp.zeros_like(gp)
    place = lax.broadcasted_iota(jnp.int32, (slots, 128), 0)
    number = lax.broadcasted_iota(jnp.int32, (2 * experts, slots), 0)

    def step(b, carry):
        hot = []
        for j in range(4):
            d = b * 4 + j
            source = (me + n - d) % n

            @pl.when(d > 0)
            def _():
                remote(dx_ref.at[source], back.at[d], ss.at[d], rs.at[d], {"dp": source}).wait_recv()

            hot.append(slot_matrix(idx_ref, source * slots, slots))
            extra = back[d, :, 0:128].astype(F32)
            high = jnp.sum(jnp.where(place == half, extra, 0.0), axis=0, keepdims=True)[:, 0:slots]
            low = jnp.sum(jnp.where(place == half + 1, extra, 0.0), axis=0, keepdims=True)[:, 0:slots]
            rows = jnp.where(number == source, high, jnp.where(number == source + experts, low, 0.0))
            gp[...] += mm(rows.astype(BF), hot[j], 1, 0)
        block = back[pl.ds(b * 4, 4)].reshape(4 * slots, D)
        acc[...] += mm(jnp.concatenate(hot, axis=0), block, 0, 0)
        return carry

    lax.fori_loop(0, n // 4, step, 0)
    copies = []
    own[own.shape[0] - 16 :, :] = jnp.zeros((16, D), BF)
    for c, (start, size) in enumerate(row_chunks(own.shape[0])):
        stop = min(start + size, tok)
        own[start:stop, :] = acc[start:stop, :].astype(BF)
        rows = pl.ds(start, size)
        copy = remote(own.at[rows, :], other.at[rows, :], hs.at[c], hr.at[c], sibling)
        copy.start()
        copies.append(copy)
    copy = remote(gp, gp_other, hs.at[len(copies)], hr.at[len(copies)], sibling)
    copy.start()
    copy.wait()
    probs = prob_ref[...]
    both = gp[...] + gp_other[...]
    grad_probs = both[0:experts, :] + both[experts:, :]
    logits = (probs * (grad_probs - jnp.sum(grad_probs * probs, axis=0, keepdims=True))).astype(BF)
    gains = jnp.transpose(small_ref[...].astype(F32))
    gain = gains[experts + 1 : experts + 2, :]
    acc[...] = mm(logits, gains[0:experts, :].astype(BF), 0, 0)
    sg_ref[...] = jnp.zeros_like(sg_ref)
    sg_ref[0:experts, :] = mm(logits, n2_ref[...], 1, 0)
    gain_sum = jnp.zeros((1, D), F32)
    bias_sum = jnp.zeros((1, D), F32)
    for c, (start, size) in enumerate(row_chunks(own.shape[0])):
        stop = min(start + size, tok)
        copies[c].wait_recv()
        grad = own[start:stop, :].astype(F32) + other[start:stop, :].astype(F32) + acc[start:stop, :]
        xhat, inverse = norm_rows(hid_ref[start:stop, :])
        hidden = ct_ref[start:stop, :].astype(F32) + norm_back(grad, gain, xhat, inverse)
        hg_ref[start:stop, :] = hidden
        gain_sum += jnp.sum(grad * xhat, axis=0, keepdims=True)
        bias_sum += jnp.sum(hidden, axis=0, keepdims=True)
    sg_ref[experts : experts + 1, :] = gain_sum
    sg_ref[experts + 1 : experts + 2, :] = bias_sum
    for copy in copies:
        copy.wait_send()

    def finish(d, carry):
        peer = (me + d) % n
        remote(dx_ref.at[peer], back.at[d], ss.at[d], rs.at[d], {"dp": peer}).wait_send()
        return carry

    lax.fori_loop(1, n, finish, 0)


def give_back(dx, idx, probs, n2, hid, ct, small, n, half):
    slots = dx.shape[1]
    experts, lanes = probs.shape
    tr = up(ct.shape[0], 16)
    chunks = len(row_chunks(tr))
    sem = pltpu.SemaphoreType.DMA
    return pl.pallas_call(
        functools.partial(return_kernel, n, half),
        out_shape=(
            jax.ShapeDtypeStruct(ct.shape, F32),
            jax.ShapeDtypeStruct((128, D), F32),
        ),
        in_specs=[whole()] * 7,
        out_specs=(whole(),) * 2,
        scratch_shapes=[
            pltpu.VMEM((n, slots, D), BF),
            pltpu.VMEM((lanes, D), F32),
            pltpu.VMEM((tr, D), BF),
            pltpu.VMEM((tr, D), BF),
            pltpu.VMEM((2 * experts, lanes), F32),
            pltpu.VMEM((2 * experts, lanes), F32),
            sem((n,)), sem((n,)), sem((chunks + 1,)), sem((chunks + 1,)),
        ],
        compiler_params=params(collective_id=2, has_side_effects=True),
        name="give_back",
    )(dx, idx, probs, n2, hid, ct, small)


def attend_back_kernel(
    experts, hg_ref, tok_ref, small_ref, w_ref, qkv_ref, att_ref, dn_ref, dw_ref,
    normed, low, dqkv, pp,
):
    images = normed.shape[0]
    scale = HD ** (-0.5)
    gains = jnp.transpose(small_ref[...].astype(F32))
    gain = gains[experts : experts + 1, :]
    tail = jnp.zeros((images, 16, D), F32)
    pp[:, SEQ_PAD - 16 : SEQ_PAD, :] = tail
    for i in range(images):
        pp[i, 0:SEQ, :] = hg_ref[i * SEQ : (i + 1) * SEQ, :]
    low[...] = pp[...].astype(BF)
    for i in range(images):
        pp[i, 0:SEQ, :] = tok_ref[i * SEQ : (i + 1) * SEQ, :].astype(F32)
    lane = lax.broadcasted_iota(jnp.int32, (1, 2 * HD), 1)
    masks = [jnp.where(lane // HD == h, 1.0, 0.0).astype(BF) for h in range(2)]
    valid = lax.broadcasted_iota(jnp.int32, (1, SEQ_PAD), 1) < SEQ

    def image(i, carry):
        xhat, _ = norm_rows(pp[i])
        normed[i] = (xhat * gain).astype(BF)
        grad_att = mm(low[i], w_ref[3], 1, 0).astype(BF)
        for p in range(w_ref.shape[2] // (2 * HD)):
            cols = slice(p * 2 * HD, (p + 1) * 2 * HD)
            q, k, v = (qkv_ref[c, i, :, cols] for c in range(3))
            pair = grad_att[:, cols]
            grads = []
            for h in range(2):
                scores = mm(q * masks[h], k, 1, 1) * scale
                scores = jnp.where(valid, scores, -1e30)
                raised = jnp.exp(scores - jnp.max(scores, axis=-1, keepdims=True))
                weights = raised / jnp.sum(raised, axis=-1, keepdims=True)
                grad_weights = mm(pair * masks[h], v, 1, 1)
                grad_scores = weights * (
                    grad_weights - jnp.sum(grad_weights * weights, axis=-1, keepdims=True)
                )
                scores_low = grad_scores.astype(BF)
                grads.append((
                    mm(scores_low, k, 1, 0) * scale,
                    mm(scores_low, q, 0, 0) * scale,
                    mm(weights.astype(BF), pair, 0, 0),
                ))
            for c in range(3):
                dqkv[c, i, :, cols] = jnp.where(lane < HD, grads[0][c], grads[1][c]).astype(BF)
        total = mm(dqkv[0, i], w_ref[0], 1, 1)
        for c in range(1, 3):
            total += mm(dqkv[c, i], w_ref[c], 1, 1)
        pp[i] = total
        return carry

    lax.fori_loop(0, images, image, 0)
    for i in range(images):
        dn_ref[i * SEQ : (i + 1) * SEQ, :] = pp[i, 0:SEQ, :]
    rows = images * SEQ_PAD

    def weight(r, carry):
        at = pl.ds(pl.multiple_of(r * 256, 256), 256)
        left = normed[:, :, at].reshape(rows, 256)
        for c in range(3):
            dw_ref[c, at, :] = mm(left, dqkv[c].reshape(rows, -1), 0, 0).astype(BF)
        left = low[:, :, at].reshape(rows, 256)
        dw_ref[3, at, :] = mm(left, att_ref[...].reshape(rows, -1), 0, 0).astype(BF)
        return carry

    lax.fori_loop(0, D // 256, weight, 0)


def attend_back(hg, tok, small, w, qkv, att, experts):
    images = tok.shape[0] // SEQ
    width = w.shape[2]
    return pl.pallas_call(
        functools.partial(attend_back_kernel, experts),
        out_shape=(
            jax.ShapeDtypeStruct(tok.shape, F32),
            jax.ShapeDtypeStruct((4, D, width), BF),
        ),
        in_specs=[whole()] * 6,
        out_specs=(whole(),) * 2,
        scratch_shapes=[
            pltpu.VMEM((images, SEQ_PAD, D), BF),
            pltpu.VMEM((images, SEQ_PAD, D), BF),
            pltpu.VMEM((3, images, SEQ_PAD, width), BF),
            pltpu.VMEM((images, SEQ_PAD, D), F32),
        ],
        compiler_params=params(),
        name="attend_back",
    )(hg, tok, small, w, qkv, att)


def last_kernel(
    n, experts, dw_ref, sg_ref, dn_ref, tok_ref, hg_ref, small_ref, y_ref, idx_ref, hid_ref,
    tg_ref, out_ref, gw_ref, gs_ref,
    own, other, mix, mix_other, sm, r1, q1, s1, t1, r2, q2, acc, hs, hr, as_, ar, bs, br,
):
    me, mine = lax.axis_index("dp"), lax.axis_index("mp")
    plane = n // LINE
    z, q = me // plane, me % plane
    tok = tok_ref.shape[0]
    rp = dw_ref.shape[3]
    sibling = {"mp": 1 - mine}
    zpeer = [((z + d) % LINE) * plane + q for d in range(1, LINE)]
    qpeer = [z * plane + (q + d) % plane for d in range(1, plane)]
    greet([sibling] + [{"dp": p} for p in zpeer + qpeer])
    sends = []
    for d, p in enumerate(qpeer):
        c = remote(dw_ref.at[:, :, (q + d + 1) % plane], r1.at[d], as_.at[d, 0], ar.at[d, 0], {"dp": p})
        c.start()
        sends.append(c)
    copies = []
    own[own.shape[0] - 16 :, :] = jnp.zeros((16, D), BF)
    for c, (start, size) in enumerate(row_chunks(own.shape[0])):
        stop = min(start + size, tok)
        own[start:stop, :] = dn_ref[start:stop, :].astype(BF)
        rows = pl.ds(start, size)
        copy = remote(own.at[rows, :], other.at[rows, :], hs.at[c], hr.at[c], sibling)
        copy.start()
        copies.append(copy)
    gains = jnp.transpose(small_ref[...].astype(F32))
    gain = gains[experts : experts + 1, :]
    gain_sum = jnp.zeros((1, D), F32)
    for c, (start, size) in enumerate(row_chunks(own.shape[0])):
        stop = min(start + size, tok)
        copies[c].wait()
        grad = own[start:stop, :].astype(F32) + other[start:stop, :].astype(F32)
        xhat, inverse = norm_rows(tok_ref[start:stop, :].astype(F32))
        tg_ref[start:stop, :] = (hg_ref[start:stop, :] + norm_back(grad, gain, xhat, inverse)).astype(BF)
        gain_sum += jnp.sum(grad * xhat, axis=0, keepdims=True)
    row = lax.broadcasted_iota(jnp.int32, sg_ref.shape, 0)
    rows = jnp.where(row == experts + 2, gain_sum, sg_ref[...])
    turned = jnp.transpose(rows).astype(BF)
    real = turned.shape[0] // n
    for b in range(n):
        at = (b // plane, b % plane)
        if real < rp:
            sm[at[0], at[1]] = jnp.zeros((rp, 128), BF)
        sm[at[0], at[1], 0:real, :] = turned[b * real : (b + 1) * real, :]
    for d, p in enumerate(qpeer):
        c = remote(sm.at[:, (q + d + 1) % plane], q1.at[d], as_.at[d, 1], ar.at[d, 1], {"dp": p})
        c.start()
        sends.append(c)
    slots = y_ref.shape[1]
    acc[...] = jnp.zeros_like(acc)

    def step(b, carry):
        hot = slot_matrix(idx_ref, b * 4 * slots, 4 * slots)
        acc[...] += mm(hot, y_ref[pl.ds(b * 4, 4)].reshape(4 * slots, D), 0, 0)
        return carry

    lax.fori_loop(0, n // 4, step, 0)
    mix[mix.shape[0] - 16 :, :] = jnp.zeros((16, D), BF)
    base = len(copies)
    late = []
    for c, (start, size) in enumerate(row_chunks(own.shape[0])):
        stop = min(start + size, tok)
        mix[start:stop, :] = acc[start:stop, :].astype(BF)
        rows = pl.ds(start, size)
        copy = remote(mix.at[rows, :], mix_other.at[rows, :], hs.at[base + c], hr.at[base + c], sibling)
        copy.start()
        late.append(copy)
    for c, (start, size) in enumerate(row_chunks(own.shape[0])):
        stop = min(start + size, tok)
        late[c].wait()
        both = mix[start:stop, :].astype(F32) + mix_other[start:stop, :].astype(F32)
        out_ref[start:stop, :] = (hid_ref[start:stop, :] + both).astype(BF)
    for d in range(plane - 1):
        remote(dw_ref.at[:, :, 0], r1.at[d], as_.at[d, 0], ar.at[d, 0], {"dp": qpeer[0]}).wait_recv()
        remote(sm.at[:, 0], q1.at[d], as_.at[d, 1], ar.at[d, 1], {"dp": qpeer[0]}).wait_recv()
    for b in range(LINE):
        value = dw_ref[:, b, q].astype(F32)
        little = sm[b, q].astype(F32)
        for d in range(plane - 1):
            value += r1[d, :, b].astype(F32)
            little += q1[d, b].astype(F32)
        s1[b] = value.astype(BF)
        t1[b] = little.astype(BF)
    for d, p in enumerate(zpeer):
        to = (z + d + 1) % LINE
        for i, (a, b) in enumerate(((s1, r2), (t1, q2))):
            c = remote(a.at[to], b.at[d], bs.at[d, i], br.at[d, i], {"dp": p})
            c.start()
            sends.append(c)
    value = s1[z].astype(F32)
    little = t1[z].astype(F32)
    for d in range(LINE - 1):
        for i, (a, b) in enumerate(((s1, r2), (t1, q2))):
            remote(a.at[0], b.at[d], bs.at[d, i], br.at[d, i], {"dp": zpeer[0]}).wait_recv()
        value += r2[d].astype(F32)
        little += q2[d].astype(F32)
    gw_ref[...] = value
    gs_ref[...] = little
    for c in sends:
        c.wait_send()


def last(dw, sg, dn, tok, hg, small, y, idx, hid, n, experts):
    parts, _, rows, width = dw.shape
    rp = rows
    plane = n // LINE
    dw = dw.reshape(parts, LINE, plane, rp, width)
    tr = up(tok.shape[0], 16)
    chunks = len(row_chunks(tr))
    sem = pltpu.SemaphoreType.DMA
    vmem = pltpu.VMEM
    return pl.pallas_call(
        functools.partial(last_kernel, n, experts),
        out_shape=(
            jax.ShapeDtypeStruct(tok.shape, BF),
            jax.ShapeDtypeStruct(tok.shape, BF),
            jax.ShapeDtypeStruct((parts, rp, width), F32),
            jax.ShapeDtypeStruct((rp, 128), F32),
        ),
        in_specs=[whole()] * 9,
        out_specs=(whole(),) * 4,
        scratch_shapes=[
            vmem((tr, D), BF), vmem((tr, D), BF), vmem((tr, D), BF), vmem((tr, D), BF),
            vmem((LINE, plane, rp, 128), BF),
            vmem((plane - 1, parts, LINE, rp, width), BF),
            vmem((plane - 1, LINE, rp, 128), BF),
            vmem((LINE, parts, rp, width), BF),
            vmem((LINE, rp, 128), BF),
            vmem((LINE - 1, parts, rp, width), BF),
            vmem((LINE - 1, rp, 128), BF),
            vmem((idx.shape[1], D), F32),
            sem((2 * chunks,)), sem((2 * chunks,)),
            sem((plane - 1, 2)), sem((plane - 1, 2)), sem((LINE - 1, 2)), sem((LINE - 1, 2)),
        ],
        compiler_params=params(collective_id=3, has_side_effects=True),
        name="last",
    )(dw, sg, dn, tok, hg, small, y, idx, hid)


def body(
    tokens, ln1_gain, w_qkv, w_out, out_bias, ln2_gain, router, w_in, in_bias,
    w_back, back_bias, routes, priority, cotangent,
):
    n = lax.axis_size("dp")
    tok = tokens.shape[0]
    experts = router.shape[1]
    cap = max(2, 5 * tok // (2 * experts))
    half = (cap + 1) // 2
    slots = up(half + FREE, 16)
    lanes = up(tok, 128)
    shard, width = w_qkv.shape[0], w_qkv.shape[2]
    rp = up(shard, 16)
    swap = [(0, 1), (1, 0)]

    wi = (w_in[0], lax.ppermute(w_in[0], "mp", swap))
    wb = (w_back[0], lax.ppermute(w_back[0], "mp", swap))
    bi = (in_bias, lax.ppermute(in_bias, "mp", swap))

    rt = jnp.pad(routes.T, ((0, 0), (0, lanes - tok)), constant_values=-1)
    ranks = jnp.pad(priority[0], (0, lanes - tok), constant_values=1 << 20)
    idx, ct_rows = route(ranks[None, :], ranks[:, None], rt, cotangent, experts, cap, half, slots)

    weights = jnp.concatenate([jnp.swapaxes(w_qkv, 0, 1), w_out.T[None]], axis=0)
    small = jnp.concatenate(
        [router, ln1_gain[:, None], ln2_gain[:, None], out_bias[:, None],
         jnp.zeros((shard, 128 - experts - 3), BF)], axis=1,
    )
    if rp > shard:
        weights = jnp.pad(weights, ((0, 0), (0, rp - shard), (0, 0)))
        small = jnp.pad(small, ((0, rp - shard), (0, 0)))
    weights, small = gather_weights(weights, small, n)
    if rp > shard:
        weights = weights.reshape(4, n, rp, width)[:, :, :shard].reshape(4, D, width)
        small = small.reshape(n, rp, 128)[:, :shard].reshape(D, 128)

    ct_rows, small = lax.optimization_barrier((ct_rows, small))
    ct_rows = lax.all_to_all(ct_rows, "dp", split_axis=0, concat_axis=0, tiled=True)

    qkv, att, part = attend(tokens, small, weights, experts)
    hid, n2, probs, x = dispatch(part, tokens, small, idx, n, experts, half, slots)
    rows = n * slots
    gi_own, gi_sib, gb_own, gb_sib, gbi_own, gbi_sib, gbb, dx, y = expert(
        x.reshape(rows, D), ct_rows.reshape(rows, D), wi, wb, bi, back_bias, n, half, slots
    )
    y = lax.all_to_all(y.reshape(n, slots, D), "dp", split_axis=0, concat_axis=0, tiled=True)
    gi_sib = lax.ppermute(gi_sib, "mp", swap)
    gb_sib = lax.ppermute(gb_sib, "mp", swap)
    little = jnp.concatenate([gbi_sib, gbb], axis=1)
    little = lax.ppermute(little, "mp", swap)
    hidden = gbi_own.shape[1]
    hg, sg = give_back(dx.reshape(n, slots, D), idx, probs, n2, hid, cotangent, small, n, half)
    dn, dw = attend_back(hg, tokens, small, weights, qkv, att, experts)
    dw = dw.reshape(4, n, shard, width)
    if rp > shard:
        dw = jnp.pad(dw, ((0, 0), (0, 0), (0, rp - shard), (0, 0)))
    tg, out, gw, gs = last(dw, sg, dn, tokens, hg, small, y, idx, hid, n, experts)
    gw, gs = gw[:, :shard], gs[:shard]
    return (
        out,
        tg,
        gs[:, experts + 2],
        jnp.swapaxes(gw[:3], 0, 1),
        gw[3].T,
        gs[:, experts + 1],
        gs[:, experts],
        gs[:, :experts],
        (gi_own + gi_sib.astype(F32))[None],
        gbi_own + little[:, :hidden],
        (gb_own + gb_sib.astype(F32))[None],
        gbb + little[:, hidden:],
    )


def solution(mesh):
    return jax.shard_map(
        body,
        mesh=mesh,
        in_specs=(
            P("dp", None),
            P("dp"),
            P("dp", None, "mp"),
            P("mp", "dp"),
            P("dp"),
            P("dp"),
            P("dp", None),
            P("dp", None, "mp"),
            P("dp", "mp"),
            P("dp", "mp", None),
            P("dp", None),
            P("dp", None),
            P("dp", None),
            P("dp", None),
        ),
        out_specs=(
            P("dp", None),
            P("dp", None),
            P("dp"),
            P("dp", None, "mp"),
            P("mp", "dp"),
            P("dp"),
            P("dp"),
            P("dp", None),
            P("dp", None, "mp"),
            P("dp", "mp"),
            P("dp", "mp", None),
            P("dp", None),
        ),
        check_vma=False,
    )
```

time: 1140 us -> 431 us (0.38); the launches traced: 1120 us -> 428 us
  waiting for transfers between devices: 382 us -> 0.02 us
  Pallas kernels: 0 us -> 373 us
  blocking collectives: 233 us -> 0 us
  local copies, waits for them, and re-layouts: 233 us -> 19.4 us
  matrix products: 156 us -> 0 us
  other arithmetic: 76.8 us -> 13.5 us
  between operations: 16.7 us -> 0.81 us
    pallas_call x0 -> x8, Pallas kernels: none -> 373 us  [the longest x1 94.7 us: give_back(): pl.pallas_call(functools.partial(return_kernel, n, half), out_shape=(jax....]
    reduce_scatter x4 -> x0, waiting for transfers between devices: 211 us -> none  [the longest x1 139 us: body(): lax.psum_scatter(grad_w_qkv, 'dp', scatter_dimension=0, tiled=True)]
    dot_general x20 -> x0, matrix products: 153 us -> none  [the longest x5 42.7 us: contract_last(): lax.dot_general(left, right, (((1,), (1,)), ((), ())), preferred_element_...]
    all_gather x2 -> x0, blocking collectives: 95.9 us -> none  [the longest x1 58.8 us: body(): part_router = lax.all_gather(router, 'dp', axis=0, tiled=True)]
    unnamed x2 -> x0, blocking collectives: 86.3 us -> none
    all_to_all x3 -> x2, waiting for transfers between devices: 84.2 us -> 0.01 us  [the longest x1 0.01 us: body(): lax.all_to_all(ct_rows, 'dp', split_axis=0, concat_axis=0, tiled=True)]
    unnamed x13 -> x0, waiting for transfers between devices: 64.2 us -> none
    gather x6 -> x0, local copies, waits for them, and re-layouts: 61.5 us -> none  [the longest x1 12.6 us: body(): picked = padded_back[slot_index].astype(jnp.float32)]
  transfers between devices with their start and end apart: 15 -> 8, of which waited for: 7 -> 0; matrix products, arithmetic and copies ran while one was open for 23% -> 3% of each run, Pallas kernels for 0% -> 49%
where the time goes in v1:
time: 431 us; the launch traced here: 428 us
  Pallas kernels  373 us (87%)
  starting transfers between devices  21.4 us (5%)
  local copies, waits for them, and re-layouts  19.4 us (5%)
  other arithmetic  13.5 us (3%)
    pallas_call x1, Pallas kernels, give_back(): pl.pallas_call(functools.partial(return_kernel, n, half), out_shape=(jax....  94.7 us
    pallas_call x1, Pallas kernels, dispatch(): pl.pallas_call(functools.partial(dispatch_kernel, n, half), out_shape=(ja...  68.1 us
    pallas_call x1, Pallas kernels, expert(): pl.pallas_call(functools.partial(expert_kernel, n, half, slots), grid=(2...  63.9 us
    pallas_call x1, Pallas kernels, last(): pl.pallas_call(functools.partial(last_kernel, n, experts), out_shape=(jax...  58.1 us
    pallas_call x1, Pallas kernels, gather_weights(): pl.pallas_call(functools.partial(gather_kernel, n), out_shape=(jax.ShapeD...  34.3 us
    pallas_call x1, Pallas kernels, attend_back(): pl.pallas_call(functools.partial(attend_back_kernel, experts), out_shape=...  32.3 us
    pallas_call x1, Pallas kernels, attend(): pl.pallas_call(functools.partial(attend_kernel, experts), out_shape=(jax....  14.5 us
    all_to_all x1, starting transfers between devices, body(): lax.all_to_all(y.reshape(n, slots, D), 'dp', split_axis=0, concat_axis=0,...  9.1 us
  transfers between devices with their start and end apart: 8, of which 0 were waited for; matrix products, arithmetic and copies ran while one was open for 3% of the time, Pallas kernels for 49%

profile of v1, /device:TPU:9, one launch (start us, length us, event | category | flops | bytes accessed | tf_op | source)
XLA Modules:
  0.0 427.8 jit_solution(1461015787685401150)
XLA Ops:
  4.4 1.0 copy.31.pcol_ref
  5.4 1.3 pad.9.rt_ref
  6.7 1.6 pad_maximum_fusion.w_ref
  9.0 34.3 %gather_weights.1 = (bf16[4,768,384]{2,1,0:T(8,128)(2,1)}, bf16[768,128]{1,0:T(8,128)(2,1)}) custom-call(bf16[4,48,384]{2,1,0:T(8,128)(2,1)} %pad_maximum_fusion.w_ref, bf16[48,128]{1,0:T(8,128)(2,1)} %concatenate.10.s_ref), custom_call_target="tpu_custom_call" | custom-call | tf_op jit(solution)/shard_map/gather_weights/pallas_call | solution.py:181
  43.3 6.8 %route.1 = (s32[2,1024]{1,0:T(2,128)}, bf16[16,80,768]{2,1,0:T(8,128)(2,1)}) custom-call(s32[1,1024]{1,0:T(1,128)} %bitcast.43, s32[1024,1]{1,0:T(8,128)} %copy.31.pcol_ref, s32[2,1024]{1,0:T(2,128)} %pad.9.rt_ref, bf16[985,768]{1,0:T(8,128)(2,1)} %ct_ref.3), custom_call_target="tpu_custom_call" | custom-call | tf_op jit(solution)/shard_map/route/pallas_call | solution.py:115
  50.1 5.2 %all-to-all-start = ((bf16[16,80,768]{2,1,0:T(8,128)(2,1)}), bf16[16,80,768]{2,1,0:T(8,128)(2,1)S(1)}, u32[]{:S(2)}, u32[]{:S(2)}) async-start(bf16[16,80,768]{2,1,0:T(8,128)(2,1)} %get-tuple-element.49), calls=%async_computation | async-start | bytes 3932160 | tf_op jit(solution)/shard_map/all_to_all | solution.py:926
  55.3 2.7 collective-permute-start
  58.6 14.5 %attend.1 = (bf16[3,5,208,384]{3,2,1,0:T(8,128)(2,1)}, bf16[5,208,384]{2,1,0:T(8,128)(2,1)}, f32[985,768]{1,0:T(8,128)}) custom-call(bf16[985,768]{1,0:T(8,128)(2,1)} %tok_ref.7, bf16[768,128]{1,0:T(8,128)(2,1)} %get-tuple-element.44.small_ref, bf16[4,768,384]{2,1,0:T(8,128)(2,1)} %get-tuple-element.45.w_ref), custom_call_target="tpu_custom_call" | custom-call | tf_op jit(solution)/shard_map/attend/pallas_call | solution.py:237
  73.1 68.1 %dispatch.1 = (f32[985,768]{1,0:T(8,128)}, bf16[1024,768]{1,0:T(8,128)(2,1)}, f32[16,1024]{1,0:T(8,128)}, bf16[16,80,768]{2,1,0:T(8,128)(2,1)}) custom-call(f32[985,768]{1,0:T(8,128)} %get-tuple-element.46.part_ref, bf16[985,768]{1,0:T(8,128)(2,1)} %tok_ref.7, bf16[768,128]{1,0:T(8,128)(2,1)} %get-tuple-element.44.small_ref, s32[2,1024]{1,0:T(2,128)} %get-tuple-element.47.idx_ref), custom_call_target="tpu_custom_call" | custom-call | tf_op jit(solution)/shard_map/dispatch/pallas_call | solution.py:338
  142.5 63.9 %expert.1 = (f32[768,1536]{1,0:T(8,128)}, bf16[768,1536]{1,0:T(8,128)(2,1)}, f32[1536,768]{1,0:T(8,128)}, bf16[1536,768]{1,0:T(8,128)(2,1)}, f32[1,1536]{1,0:T(1...) custom-call(bf16[1280,768]{1,0:T(8,128)(2,1)} %bitcast.37, ...), custom_call_target="tpu_custom_call" | custom-call | tf_op jit(solution)/shard_map/expert/pallas_call | solution.py:511
  206.4 3.1 collective-permute-start.3
  209.6 9.1 %all-to-all-start.1 = ((bf16[16,80,768]{2,1,0:T(8,128)(2,1)}), bf16[16,80,768]{2,1,0:T(8,128)(2,1)S(1)}, u32[]{:S(2)}, u32[]{:S(2)}) async-start(bf16[16,80,768]{2,1,0:T(8,128)(2,1)} %bitcast.38), calls=%async_computation.1 | async-start | bytes 3932160 | tf_op jit(solution)/shard_map/all_to_all | solution.py:934
  219.4 94.7 %give_back.1 = (f32[985,768]{1,0:T(8,128)}, f32[128,768]{1,0:T(8,128)}) custom-call(bf16[16,80,768]{2,1,0:T(8,128)(2,1)} %bitcast.39, s32[2,1024]{1,0:T(2,128)} %get-tuple-element.47.idx_ref, f32[16,1024]{1,0:T(8,128)} %get-tuple-element.51.prob_ref, bf16[1024,768]{1,0:T(8,128)(2,1)} %get-tuple-element.52.n2_ref, f32[985,768]{1,0:T(8,128)} %get-tuple-element.53.hid_ref, ...), custom_call_target="tpu_custom_call" | custom-call | tf_op jit(solution)/shard_map/give_back/pallas_call | solution.py:635
  314.1 32.3 %attend_back.1 = (f32[985,768]{1,0:T(8,128)}, bf16[4,768,384]{2,1,0:T(8,128)(2,1)}) custom-call(f32[985,768]{1,0:T(8,128)} %get-tuple-element.54.hg_ref, bf16[985,768]{1,0:T(8,128)(2,1)} %tok_ref.7, bf16[768,128]{1,0:T(8,128)(2,1)} %get-tuple-element.44.small_ref, bf16[4,768,384]{2,1,0:T(8,128)(2,1)} %get-tuple-element.45.w_ref, ...), custom_call_target="tpu_custom_call" | custom-call | tf_op jit(solution)/shard_map/attend_back/pallas_call | solution.py:728
  347.6 6.1 %add_bitcast_fusion.1 = f32[1,768,1536]{2,1,0:T(8,128)} fusion(f32[768,1536]{1,0:T(8,128)} %get-tuple-element.65, bf16[768,1536]{1,0:T(8,128)(2,1)} %collective-permute-done.3), kind=kLoop, calls=%fused_computation.1 | loop fusion | flops 2359296 | bytes 11796480 | tf_op jit(solution)/shard_map/broadcast_in_dim | solution.py:956
  353.8 4.6 %add_bitcast_fusion = f32[1,1536,768]{2,1,0:T(8,128)} fusion(f32[1536,768]{1,0:T(8,128)S(1)} %bitcast.31, bf16[1536,768]{1,0:T(8,128)(2,1)} %collective-permute-done.5), kind=kLoop, calls=%fused_computation | loop fusion | flops 2359296 | bytes 11796480 | tf_op jit(solution)/shard_map/broadcast_in_dim | solution.py:958
  358.4 1.3 copy-done.1
  359.7 58.1 %last.1 = (bf16[985,768]{1,0:T(8,128)(2,1)}, bf16[985,768]{1,0:T(8,128)(2,1)}, f32[4,48,384]{2,1,0:T(8,128)}, f32[48,128]{1,0:T(8,128)}) custom-call(bf16[4,4,4,48,384]{4,3,2,1,0:T(8,128)(2,1)} %bitcast.36, f32[128,768]{1,0:T(8,128)} %get-tuple-element.58.sg_ref, f32[985,768]{1,0:T(8,128)} %get-tuple-element.59.dn_ref, bf16[985,768]{1,0:T(8,128)(2,1)} %tok_ref.7, ...), custom_call_target="tpu_custom_call" | custom-call | tf_op jit(solution)/shard_map/last/pallas_call | solution.py:861
  417.8 1.6 slice_bitcast_fusion.1
  419.4 1.6 slice_bitcast_fusion
  421.1 1.6 slice_reduce_fusion
  422.7 1.4 copy.36
  424.1 2.6 copy.39
  426.7 1.1 copy.40
  (44 shorter events, 8.2 us)
Async XLA Ops:
  4.4 38.9 %copy-start.3 = (s32[1024]{0:T(1024)}, s32[1024]{0:T(1024)S(1)}, u32[]{:S(2)}) copy-start(s32[1024]{0:T(1024)S(1)} %pad.8) | copy-start | bytes 12292
  50.1 8.0 %copy-start.5 = (bf16[1,1536]{1,0:T(2,128)(2,1)S(1)}, bf16[1,1536]{1,0:T(2,128)(2,1)}, u32[]{:S(2)}) copy-start(bf16[1,1536]{1,0:T(2,128)(2,1)} %bi_own.1) | copy-start | bytes 9220
  50.1 91.1 %all-to-all-start = ((bf16[16,80,768]{2,1,0:T(8,128)(2,1)}), bf16[16,80,768]{2,1,0:T(8,128)(2,1)S(1)}, u32[]{:S(2)}, u32[]{:S(2)}) async-start(bf16[16,80,768]{2,1,0:T(8,128)(2,1)} %get-tuple-element.49), calls=%async_computation | async-start | bytes 3932160 | tf_op jit(solution)/shard_map/all_to_all | solution.py:926
  55.3 85.8 %collective-permute-start = (bf16[768,1536]{1,0:T(8,128)(2,1)}, bf16[768,1536]{1,0:T(8,128)(2,1)}, u32[]{:S(2)}, u32[]{:S(2)}) collective-permute-start(bf16[768,1536]{1,0:T(8,128)(2,1)} %bitcast.32), channel_id=1, source_target_pairs={{0,1},{1,0},{2,3},{3,2},{4,5},{5,4},{6,7},{7,6},{8,9},{9,8},{10,11... | collective-permute-start | bytes 7077896 | tf_op jit(solution)/shard_map/ppermute | solution.py:904
  58.1 83.2 %collective-permute-start.1 = (bf16[1536,768]{1,0:T(8,128)(2,1)}, bf16[1536,768]{1,0:T(8,128)(2,1)}, u32[]{:S(2)}, u32[]{:S(2)}) collective-permute-start(bf16[1536,768]{1,0:T(8,128)(2,1)} %bitcast.34), channel_id=1, source_target_pairs={{0,1},{1,0},{2,3},{3,2},{4,5},{5,4},{6,7},{7,6},{8,9},{9,8},{10,11... | collective-permute-start | bytes 7077896 | tf_op jit(solution)/shard_map/ppermute | solution.py:905
  58.1 83.0 %collective-permute-start.2 = (bf16[1,1536]{1,0:T(2,128)(2,1)S(1)}, bf16[1,1536]{1,0:T(2,128)(2,1)S(1)}, u32[]{:S(2)}, u32[]{:S(2)}) collective-permute-start(bf16[1,1536]{1,0:T(2,128)(2,1)S(1)} %copy-done.5), channel_id=1, source_target_pairs={{0,1},{1,0},{2,3},{3,2},{4,5},{5,4},{6,7},{7,6},{8,9},{9,8},{10,11... | collective-permute-start | bytes 9224 | tf_op jit(solution)/shard_map/ppermute | solution.py:906
  141.2 0.6 copy-start.6
  141.2 1.3 copy-start
  206.4 12.9 %copy-start.4 = (f32[1,768]{1,0:T(1,128)S(1)}, f32[1,768]{1,0:T(1,128)}, u32[]{:S(2)}) copy-start(f32[1,768]{1,0:T(1,128)} %get-tuple-element.69) | copy-start | bytes 9220
  206.4 12.9 %copy-start.8 = (f32[1,1536]{1,0:T(1,128)S(1)}, f32[1,1536]{1,0:T(1,128)}, u32[]{:S(2)}) copy-start(f32[1,1536]{1,0:T(1,128)} %get-tuple-element.68) | copy-start | bytes 18436
  206.4 141.2 %collective-permute-start.3 = (bf16[768,1536]{1,0:T(8,128)(2,1)}, bf16[768,1536]{1,0:T(8,128)(2,1)}, u32[]{:S(2)}, u32[]{:S(2)}) collective-permute-start(bf16[768,1536]{1,0:T(8,128)(2,1)} %get-tuple-element.66), channel_id=1, source_target_pairs={{0,1},{1,0},{2,3},{3,2},{4,5},{5,4},{6,7},{7,6},{8,9},{9,8},{10,11... | collective-permute-start | bytes 7077896 | tf_op jit(solution)/shard_map/ppermute | solution.py:935
  209.6 148.8 %all-to-all-start.1 = ((bf16[16,80,768]{2,1,0:T(8,128)(2,1)}), bf16[16,80,768]{2,1,0:T(8,128)(2,1)S(1)}, u32[]{:S(2)}, u32[]{:S(2)}) async-start(bf16[16,80,768]{2,1,0:T(8,128)(2,1)} %bitcast.38), calls=%async_computation.1 | async-start | bytes 3932160 | tf_op jit(solution)/shard_map/all_to_all | solution.py:934
  218.7 135.1 %collective-permute-start.5 = (bf16[1536,768]{1,0:T(8,128)(2,1)}, bf16[1536,768]{1,0:T(8,128)(2,1)}, u32[]{:S(2)}, u32[]{:S(2)}) collective-permute-start(bf16[1536,768]{1,0:T(8,128)(2,1)} %get-tuple-element.71), channel_id=1, source_target_pairs={{0,1},{1,0},{2,3},{3,2},{4,5},{5,4},{6,7},{7,6},{8,9},{9,8},{10,11... | collective-permute-start | bytes 7077896 | tf_op jit(solution)/shard_map/ppermute | solution.py:936
  219.3 127.1 %collective-permute-start.4 = (f32[1,2304]{1,0:T(1,128)S(1)}, f32[1,2304]{1,0:T(1,128)S(1)}, u32[]{:S(2)}, u32[]{:S(2)}) collective-permute-start(f32[1,2304]{1,0:T(1,128)S(1)} %pad_maximum_fusion.1), channel_id=1, source_target_pairs={{0,1},{1,0},{2,3},{3,2},{4,5},{5,4},{6,7},{7,6},{8,9},{9,8},{10,11... | collective-permute-start | bytes 27656 | tf_op jit(solution)/shard_map/ppermute | solution.py:938
  314.1 32.9 %copy-start.7 = (f32[1,1536]{1,0:T(1,128)S(1)}, f32[1,1536]{1,0:T(1,128)}, u32[]{:S(2)}) copy-start(f32[1,1536]{1,0:T(1,128)} %get-tuple-element.67) | copy-start | bytes 18436
  347.6 6.1 %slice-start = ((s8[4718592]{0:T(1024)(128)(4,1)}), s8[4194304]{0:T(1024)(128)(4,1)S(1)}, s32[]{:S(2)}) async-start(s8[4718592]{0:T(1024)(128)(4,1)} %bitcast.30), calls=%async_computation.2 | async-start | bytes 8388608
  347.6 6.1 %slice-start.1 = ((s8[4718592]{0:T(1024)(128)(4,1)}), s8[524288]{0:T(1024)(128)(4,1)S(1)}, s32[]{:S(2)}) async-start(s8[4718592]{0:T(1024)(128)(4,1)} %bitcast.30), calls=%async_computation.3 | async-start | bytes 1048576
  358.4 1.3 copy-start.1
  417.8 8.9 %copy-start.2 = (bf16[985,768]{1,0:T(8,128)(2,1)S(1)}, bf16[985,768]{1,0:T(8,128)(2,1)}, u32[]{:S(2)}) copy-start(bf16[985,768]{1,0:T(8,128)(2,1)} %get-tuple-element.112) | copy-start | bytes 4538884

commit v2 on v1

--- a/solution.py
+++ b/solution.py
@@ -313,16 +313,16 @@
 
             @pl.when(d > 0)
             def _():
-                remote(send.at[d], x_ref.at[me], ss.at[d], rs.at[d], {"dp": peer}).start()
+                remote(send.at[d], x_ref.at[d], ss.at[d], rs.at[d], {"dp": peer}).start()
 
         return carry
 
     lax.fori_loop(0, n // 4, step, 0)
-    x_ref[me] = send[0]
+    x_ref[0] = send[0]
 
     def finish(d, carry):
         source = (me + n - d) % n
-        remote(send.at[d], x_ref.at[source], ss.at[d], rs.at[d], {"dp": source}).wait()
+        remote(send.at[d], x_ref.at[d], ss.at[d], rs.at[d], {"dp": source}).wait()
         return carry
 
     lax.fori_loop(1, n, finish, 0)
@@ -358,235 +358,195 @@
 
 
 def expert_kernel(
-    n, half, slots,
+    n, half, experts,
     x_ref, ct_ref, wi_own, wi_sib, wb_own, wb_sib, bi_own, bi_sib, bb_ref,
-    gi_own, gi_sib, gb_own, gb_sib, gbi_own, gbi_sib, gbb_ref, dx_ref, y_ref,
-    xt, g_s, y_acc, dx_acc, act_s, dpre_s, gate_s, wi_s, wb_s,
-):
-    k, steps = pl.program_id(0), pl.num_programs(0)
-    first = k < steps // 2
-    rows_all = n * slots
-    tile = 256
-    tiles = rows_all // tile
-
-    def in_group():
-        row = lax.broadcasted_iota(jnp.int32, (tile, n), 0)
-        return row, lax.broadcasted_iota(jnp.int32, (tile, n), 1)
-
-    @pl.when(k == 0)
-    def _():
-        group = lax.broadcasted_iota(jnp.int32, (n, rows_all), 0)
-        row = lax.broadcasted_iota(jnp.int32, (n, rows_all), 1)
-        pick = jnp.where((row == group * slots + half) | (row == group * slots + half + 1), 1.0, 0.0)
-        gates = mm(pick.astype(BF), x_ref[:, 0:128], 1, 0)
-        high, low = split_two(gates)
-
-        def start(r, total):
-            at = pl.ds(pl.multiple_of(r * tile, tile), tile)
-            row, group = in_group()
-            mine = jnp.where((row + r * tile) // slots == group, 1.0, 0.0).astype(BF)
-            wide = mm(mine, high, 1, 0) + mm(mine, low, 1, 0)
-            spot = lax.broadcasted_iota(jnp.int32, (tile, 128), 0) + r * tile
-            lane = lax.broadcasted_iota(jnp.int32, (tile, 128), 1)
-            gate = jnp.sum(jnp.where(lane == spot % slots, wide, 0.0), axis=1, keepdims=True)
-            gate_s[at, :] = gate
-            scaled = (gate * ct_ref[at, :].astype(F32)).astype(BF)
-            g_s[at, :] = scaled
-            xt[:, at] = jnp.transpose(x_ref[at, :].astype(F32)).astype(BF)
-            return total + jnp.sum(scaled.astype(F32), axis=0, keepdims=True)
-
-        gbb_ref[...] = lax.fori_loop(0, tiles, start, jnp.zeros((1, D), F32))
-        y_acc[...] = jnp.zeros_like(y_acc)
-        dx_acc[...] = jnp.zeros_like(dx_acc)
-
-    @pl.when(first)
-    def _():
-        wi_s[...] = wi_own[...]
-        wb_s[...] = wb_own[...]
-
-    @pl.when(jnp.logical_not(first))
-    def _():
-        wi_s[...] = wi_sib[...]
-        wb_s[...] = wb_sib[...]
-
-    bias = jnp.where(first, bi_own[...], bi_sib[...]).astype(F32)
-
-    def forward(r, total):
-        at = pl.ds(pl.multiple_of(r * tile, tile), tile)
-        pre = mm(x_ref[at, :], wi_s[...], 1, 0) + bias
-        phi = 0.5 * (1.0 + lax.erf(pre * (0.5**0.5)))
-        slope = phi + pre * (jnp.exp(-0.5 * pre * pre) * ((2.0 * jnp.pi) ** -0.5))
-        act = (pre * phi).astype(BF)
-        act_s[at, :] = act
-        grad = (mm(g_s[at, :], wb_s[...], 1, 1) * slope).astype(BF)
-        dpre_s[at, :] = grad
-        y_acc[at, :] += mm(act, wb_s[...], 1, 0)
-        dx_acc[at, :] += mm(grad, wi_s[...], 1, 1)
-        return total + jnp.sum(grad.astype(F32), axis=0, keepdims=True)
-
-    total = lax.fori_loop(0, tiles, forward, jnp.zeros(bias.shape, F32))
-
-    def first_weight(r, carry):
-        at = pl.ds(pl.multiple_of(r * tile, tile), tile)
-        grad = mm(xt[at, :], dpre_s[...], 1, 0)
-
-        @pl.when(first)
-        def _():
-            gi_own[at, :] = grad
-
-        @pl.when(jnp.logical_not(first))
-        def _():
-            gi_sib[at, :] = grad.astype(BF)
-
-        return carry
-
-    lax.fori_loop(0, D // tile, first_weight, 0)
-
-    def second_weight(r, carry):
-        at = pl.ds(pl.multiple_of(r * tile, tile), tile)
-        grad = mm(act_s[:, at], g_s[...], 0, 0)
-
-        @pl.when(first)
-        def _():
-            gb_own[at, :] = grad
-
-        @pl.when(jnp.logical_not(first))
-        def _():
-            gb_sib[at, :] = grad.astype(BF)
-
-        return carry
-
-    lax.fori_loop(0, act_s.shape[1] // tile, second_weight, 0)
-
-    @pl.when(first)
-    def _():
-        gbi_own[...] = total
-
-    @pl.when(jnp.logical_not(first))
-    def _():
-        gbi_sib[...] = total
-
-    @pl.when(k == steps - 1)
-    def _():
-        def finish(r, sums):
-            at = pl.ds(pl.multiple_of(r * tile, tile), tile)
-            y = (y_acc[at, :] + bb_ref[...].astype(F32)).astype(BF).astype(F32)
-            y_ref[at, :] = (gate_s[at, :] * y).astype(BF)
-            dots = jnp.sum(ct_ref[at, :].astype(F32) * y, axis=1, keepdims=True)
-            spot = lax.broadcasted_iota(jnp.int32, (tile, 128), 0) + r * tile
-            lane = lax.broadcasted_iota(jnp.int32, (tile, 128), 1)
-            spread = jnp.where(lane == spot % slots, dots, 0.0)
-            row, group = in_group()
-            mine = jnp.where((row + r * tile) // slots == group, 1.0, 0.0).astype(BF)
-            high, low = split_two(spread)
-            return sums[0] + mm(mine, high, 0, 0), sums[1] + mm(mine, low, 0, 0)
-
-        zero = jnp.zeros((n, 128), F32)
-        high, low = lax.fori_loop(0, tiles, finish, (zero, zero))
-        high, low = high.astype(BF), low.astype(BF)
-
-        def leave(r, carry):
-            at = pl.ds(pl.multiple_of(r * tile, tile), tile)
-            row, group = in_group()
-            spot = row + r * tile - group * slots
-            put = [jnp.where(spot == half + i, 1.0, 0.0).astype(BF) for i in range(2)]
-            dx_ref[at, :] = dx_acc[at, :].astype(BF)
-            dx_ref[at, 0:128] = (dx_acc[at, 0:128] + mm(put[0], high, 1, 0) + mm(put[1], low, 1, 0)).astype(BF)
-            return carry
-
-        lax.fori_loop(0, tiles, leave, 0)
-
-
-def expert(x, ct, wi, wb, bi, bb, n, half, slots):
-    rows = n * slots
-    hidden = wi[0].shape[1]
-    chunk = 512
-    each = hidden // chunk
-    own = lambda k: jnp.minimum(k, each - 1)
-    sib = lambda k: jnp.maximum(k - each, 0)
-    cols = lambda at: pl.BlockSpec((D, chunk), lambda k: (0, at(k)))
-    lines = lambda at: pl.BlockSpec((chunk, D), lambda k: (at(k), 0))
-    strip = lambda at: pl.BlockSpec((1, chunk), lambda k: (0, at(k)))
-    shape = jax.ShapeDtypeStruct
-    return pl.pallas_call(
-        functools.partial(expert_kernel, n, half, slots),
-        grid=(2 * each,),
-        out_shape=(
-            shape((D, hidden), F32), shape((D, hidden), BF),
-            shape((hidden, D), F32), shape((hidden, D), BF),
-            shape((1, hidden), F32), shape((1, hidden), F32), shape((1, D), F32),
-            shape((rows, D), BF), shape((rows, D), BF),
-        ),
-        in_specs=[whole(), whole(), cols(own), cols(sib), lines(own), lines(sib), strip(own), strip(sib), whole()],
-        out_specs=(
-            cols(own), cols(sib), lines(own), lines(sib), strip(own), strip(sib), whole(), whole(), whole(),
-        ),
-        scratch_shapes=[
-            pltpu.VMEM((D, rows), BF),
-            pltpu.VMEM((rows, D), BF),
-            pltpu.VMEM((rows, D), F32),
-            pltpu.VMEM((rows, D), F32),
-            pltpu.VMEM((rows, chunk), BF),
-            pltpu.VMEM((rows, chunk), BF),
-            pltpu.VMEM((rows, 1), F32),
-            pltpu.VMEM((D, chunk), BF),
-            pltpu.VMEM((chunk, D), BF),
-        ],
-        compiler_params=params(dimension_semantics=("arbitrary",)),
-        name="expert",
-    )(x, ct, wi[0], wi[1], wb[0], wb[1], bi[0], bi[1], bb)
-
-
-def return_kernel(
-    n, half, dx_ref, idx_ref, prob_ref, n2_ref, hid_ref, ct_ref, small_ref, hg_ref, sg_ref,
-    back, acc, own, other, gp, gp_other, ss, rs, hs, hr,
+    idx_ref, prob_ref, hid_ref, tok_ct, small_ref,
+    hg_ref, sg_ref, y_ref, gi_ref, gi_in, gb_ref, gb_in, little_ref, little_in,
+    vi_own, vi_sib, vb_own, vb_sib, g_s, act_own, act_sib, dp_own, dp_sib, dx_s, back, acc, other,
+    ct_s, y_s, stage, gp, gp_other,
+    lsem, ysem, gsem, ss, rs, hs, hr, ms, mr,
 ):
     me, mine = lax.axis_index("dp"), lax.axis_index("mp")
-    tok = ct_ref.shape[0]
-    slots = dx_ref.shape[1]
-    experts = prob_ref.shape[0]
     sibling = {"mp": 1 - mine}
+    slots = x_ref.shape[1]
+    tok = tok_ct.shape[0]
+    hidden = wi_own.shape[1]
+    group = 4 * slots
+    batches = n // 4
+    loads = [
+        pltpu.make_async_copy(a, b, lsem.at[i])
+        for i, (a, b) in enumerate(
+            ((wi_own, vi_own), (wb_own, vb_own), (wi_sib, vi_sib), (wb_sib, vb_sib), (hid_ref, hg_ref))
+        )
+    ]
+    for c in loads:
+        c.start()
     greet([sibling] + [{"dp": (me + d) % n} for d in range(1, n)])
-
-    def begin(d, carry):
-        peer = (me + d) % n
-        remote(dx_ref.at[peer], back.at[d], ss.at[d], rs.at[d], {"dp": peer}).start()
+    little_ref[...] = jnp.zeros_like(little_ref)
+
+    def cts(b, j):
+        return pltpu.make_async_copy(ct_ref.at[(me + n - b * 4 - j) % n], ct_s.at[j], ysem.at[0, j])
+
+    def ys(b, j):
+        return pltpu.make_async_copy(y_s.at[j], y_ref.at[(me + n - b * 4 - j) % n], ysem.at[1, j])
+
+    for j in range(4):
+        cts(0, j).start()
+    for c in loads[:4]:
+        c.wait()
+    chunk = 768
+    row = lax.broadcasted_iota(jnp.int32, (group, 16), 0)
+    number = lax.broadcasted_iota(jnp.int32, (group, 16), 1)
+    member = jnp.where(row // slots == number, 1.0, 0.0).astype(BF)
+    spot = lax.broadcasted_iota(jnp.int32, (group, 128), 0) % slots
+    here = spot == lax.broadcasted_iota(jnp.int32, (group, 128), 1)
+    row_t = lax.broadcasted_iota(jnp.int32, (16, group), 1)
+    number_t = lax.broadcasted_iota(jnp.int32, (16, group), 0)
+    pick = jnp.where(
+        (row_t == number_t * slots + half) | (row_t == number_t * slots + half + 1), 1.0, 0.0
+    ).astype(BF)
+    member_t = jnp.where(row_t // slots == number_t, 1.0, 0.0).astype(BF)
+    puts = [jnp.where(row == number * slots + half + i, 1.0, 0.0).astype(BF) for i in range(2)]
+
+    def batch(b, carry):
+        at = pl.ds(pl.multiple_of(b * group, 16), group)
+        x = x_ref[pl.ds(b * 4, 4)].reshape(group, D)
+        high, low = split_two(mm(pick, x[:, 0:128], 1, 0))
+        wide = mm(member, high, 1, 0) + mm(member, low, 1, 0)
+        gate = jnp.sum(jnp.where(here, wide, 0.0), axis=1, keepdims=True)
+        for j in range(4):
+            cts(b, j).wait()
+        g_s[at, :] = (gate * ct_s[...].reshape(group, D).astype(F32)).astype(BF)
+        little_ref[0:1, 2 * hidden :] += jnp.sum(g_s[at, :].astype(F32), axis=0, keepdims=True)
+        for part, (vi, vb, bi, acts, dps) in enumerate(
+            ((vi_own, vb_own, bi_own, act_own, dp_own), (vi_sib, vb_sib, bi_sib, act_sib, dp_sib))
+        ):
+            for c in range(hidden // chunk):
+                cols = slice(c * chunk, (c + 1) * chunk)
+                pre = mm(x_ref[pl.ds(b * 4, 4)].reshape(group, D), vi[:, cols], 1, 0) + bi[:, cols].astype(F32)
+                phi = 0.5 * (1.0 + lax.erf(pre * (0.5**0.5)))
+                slope = phi + pre * (jnp.exp(-0.5 * pre * pre) * ((2.0 * jnp.pi) ** -0.5))
+                acts[at, cols] = (pre * phi).astype(BF)
+                grad = (mm(g_s[at, :], vb[cols, :], 1, 1) * slope).astype(BF)
+                dps[at, cols] = grad
+                place = slice(part * hidden + c * chunk, part * hidden + (c + 1) * chunk)
+                little_ref[0:1, place] += jnp.sum(grad.astype(F32), axis=0, keepdims=True)
+        dx = mm(dp_own[at, :], vi_own[...], 1, 1) + mm(dp_sib[at, :], vi_sib[...], 1, 1)
+        y = mm(act_own[at, :], vb_own[...], 1, 0) + mm(act_sib[at, :], vb_sib[...], 1, 0)
+        y = (y + bb_ref[...].astype(F32)).astype(BF).astype(F32)
+        dots = jnp.sum(ct_s[...].reshape(group, D).astype(F32) * y, axis=1, keepdims=True)
+        high, low = split_two(jnp.where(here, dots, 0.0))
+        high, low = mm(member_t, high, 1, 0).astype(BF), mm(member_t, low, 1, 0).astype(BF)
+        left = dx[:, 0:128] + mm(puts[0], high, 1, 0) + mm(puts[1], low, 1, 0)
+        dx = jnp.concatenate([left, dx[:, 128:]], axis=1)
+        dx_s[pl.ds(b * 4, 4)] = dx.astype(BF).reshape(4, slots, D)
+        for j in range(4):
+            d = b * 4 + j
+
+            @pl.when(d > 0)
+            def _():
+                remote(dx_s.at[d], back.at[d], ss.at[d], rs.at[d], {"dp": (me + n - d) % n}).start()
+
+        @pl.when(b > 0)
+        def _():
+            for j in range(4):
+                ys(b - 1, j).wait()
+
+        y_s[...] = (gate * y).astype(BF).reshape(4, slots, D)
+        for j in range(4):
+            ys(b, j).start()
+
+        @pl.when(b + 1 < batches)
+        def _():
+            for j in range(4):
+                cts(b + 1, j).start()
+
         return carry
 
-    lax.fori_loop(1, n, begin, 0)
-    back[0] = dx_ref[me]
+    lax.fori_loop(0, batches, batch, 0)
+    back[0] = dx_s[0]
+    little = remote(little_ref, little_in, ms.at[2], mr.at[2], sibling)
+    little.start()
+
+    rows_all = n * slots
+    steps = 3
+    size = D // steps
+    wide = hidden // 2
+    swaps = []
+
+    def out_i(r, c):
+        return pltpu.make_async_copy(
+            stage.at[r % 2, c * size : (c + 1) * size, :],
+            gi_ref.at[r * size : (r + 1) * size, c * wide : (c + 1) * wide], gsem.at[c, r],
+        )
+
+    def out_b(r):
+        return pltpu.make_async_copy(
+            stage.at[r % 2], gb_ref.at[r * 2 * size : (r + 1) * 2 * size, :], gsem.at[2, r]
+        )
+
+    for r in range(steps):
+        at = slice(r * size, (r + 1) * size)
+        left = x_ref[:, :, at].reshape(rows_all, size)
+        vi_sib[at, :] = mm(left, dp_sib[...], 0, 0).astype(BF)
+        for c in range(2):
+            if r >= 2:
+                out_i(r - 2, c).wait()
+            stage[r % 2, c * size : (c + 1) * size, :] = mm(left, dp_own[:, c * wide : (c + 1) * wide], 0, 0)
+            out_i(r, c).start()
+    copy = remote(vi_sib, gi_in, ms.at[0], mr.at[0], sibling)
+    copy.start()
+    swaps.append(copy)
+
     acc[...] = jnp.zeros_like(acc)
     gp[...] = jnp.zeros_like(gp)
     place = lax.broadcasted_iota(jnp.int32, (slots, 128), 0)
-    number = lax.broadcasted_iota(jnp.int32, (2 * experts, slots), 0)
-
-    def step(b, carry):
+    count = lax.broadcasted_iota(jnp.int32, (experts, slots), 0)
+
+    def combine(b, carry):
         hot = []
         for j in range(4):
             d = b * 4 + j
-            source = (me + n - d) % n
+            source = (me + d) % n
 
             @pl.when(d > 0)
             def _():
-                remote(dx_ref.at[source], back.at[d], ss.at[d], rs.at[d], {"dp": source}).wait_recv()
+                remote(dx_s.at[d], back.at[d], ss.at[d], rs.at[d], {"dp": source}).wait_recv()
 
             hot.append(slot_matrix(idx_ref, source * slots, slots))
             extra = back[d, :, 0:128].astype(F32)
             high = jnp.sum(jnp.where(place == half, extra, 0.0), axis=0, keepdims=True)[:, 0:slots]
             low = jnp.sum(jnp.where(place == half + 1, extra, 0.0), axis=0, keepdims=True)[:, 0:slots]
-            rows = jnp.where(number == source, high, jnp.where(number == source + experts, low, 0.0))
-            gp[...] += mm(rows.astype(BF), hot[j], 1, 0)
-        block = back[pl.ds(b * 4, 4)].reshape(4 * slots, D)
+            for value in (high, low):
+                gp[...] += mm(jnp.where(count == source, value, 0.0).astype(BF), hot[j], 1, 0)
+        block = back[pl.ds(b * 4, 4)].reshape(group, D)
         acc[...] += mm(jnp.concatenate(hot, axis=0), block, 0, 0)
         return carry
 
-    lax.fori_loop(0, n // 4, step, 0)
+    lax.fori_loop(0, batches // 2, combine, 0)
+    for r in range(steps):
+        at = slice(r * 2 * size, (r + 1) * 2 * size)
+        vb_sib[at, :] = mm(act_sib[:, at], g_s[...], 0, 0).astype(BF)
+        if r == 0:
+            for c in range(2):
+                out_i(1, c).wait()
+                out_i(2, c).wait()
+        if r >= 2:
+            out_b(r - 2).wait()
+        stage[r % 2] = mm(act_own[:, at], g_s[...], 0, 0)
+        out_b(r).start()
+    copy = remote(vb_sib, gb_in, ms.at[1], mr.at[1], sibling)
+    copy.start()
+    swaps.append(copy)
+    lax.fori_loop(batches // 2, batches, combine, 0)
+
     copies = []
-    own[own.shape[0] - 16 :, :] = jnp.zeros((16, D), BF)
-    for c, (start, size) in enumerate(row_chunks(own.shape[0])):
-        stop = min(start + size, tok)
+    own = g_s
+    own[other.shape[0] - 16 : other.shape[0], :] = jnp.zeros((16, D), BF)
+    for c, (start, length) in enumerate(row_chunks(other.shape[0])):
+        stop = min(start + length, tok)
         own[start:stop, :] = acc[start:stop, :].astype(BF)
-        rows = pl.ds(start, size)
+        rows = pl.ds(start, length)
         copy = remote(own.at[rows, :], other.at[rows, :], hs.at[c], hr.at[c], sibling)
         copy.start()
         copies.append(copy)
@@ -594,86 +554,118 @@
     copy.start()
     copy.wait()
     probs = prob_ref[...]
-    both = gp[...] + gp_other[...]
-    grad_probs = both[0:experts, :] + both[experts:, :]
+    grad_probs = gp[...] + gp_other[...]
     logits = (probs * (grad_probs - jnp.sum(grad_probs * probs, axis=0, keepdims=True))).astype(BF)
     gains = jnp.transpose(small_ref[...].astype(F32))
     gain = gains[experts + 1 : experts + 2, :]
     acc[...] = mm(logits, gains[0:experts, :].astype(BF), 0, 0)
     sg_ref[...] = jnp.zeros_like(sg_ref)
-    sg_ref[0:experts, :] = mm(logits, n2_ref[...], 1, 0)
     gain_sum = jnp.zeros((1, D), F32)
     bias_sum = jnp.zeros((1, D), F32)
-    for c, (start, size) in enumerate(row_chunks(own.shape[0])):
-        stop = min(start + size, tok)
+    lanes = acc.shape[0]
+    act_own[lanes - 64 : lanes, 0:D] = jnp.zeros((64, D), BF)
+    loads[4].wait()
+    for c, (start, length) in enumerate(row_chunks(other.shape[0])):
+        stop = min(start + length, tok)
         copies[c].wait_recv()
         grad = own[start:stop, :].astype(F32) + other[start:stop, :].astype(F32) + acc[start:stop, :]
-        xhat, inverse = norm_rows(hid_ref[start:stop, :])
-        hidden = ct_ref[start:stop, :].astype(F32) + norm_back(grad, gain, xhat, inverse)
-        hg_ref[start:stop, :] = hidden
+        xhat, inverse = norm_rows(hg_ref[start:stop, :])
+        act_own[start:stop, 0:D] = (xhat * gain).astype(BF)
+        hidden_grad = tok_ct[start:stop, :].astype(F32) + norm_back(grad, gain, xhat, inverse)
+        hg_ref[start:stop, :] = hidden_grad
         gain_sum += jnp.sum(grad * xhat, axis=0, keepdims=True)
-        bias_sum += jnp.sum(hidden, axis=0, keepdims=True)
+        bias_sum += jnp.sum(hidden_grad, axis=0, keepdims=True)
+    sg_ref[0:experts, :] = mm(logits, act_own[0:lanes, 0:D], 1, 0)
     sg_ref[experts : experts + 1, :] = gain_sum
     sg_ref[experts + 1 : experts + 2, :] = bias_sum
     for copy in copies:
         copy.wait_send()
 
     def finish(d, carry):
-        peer = (me + d) % n
-        remote(dx_ref.at[peer], back.at[d], ss.at[d], rs.at[d], {"dp": peer}).wait_send()
+        remote(dx_s.at[d], back.at[d], ss.at[d], rs.at[d], {"dp": (me + n - d) % n}).wait_send()
         return carry
 
     lax.fori_loop(1, n, finish, 0)
-
-
-def give_back(dx, idx, probs, n2, hid, ct, small, n, half):
-    slots = dx.shape[1]
+    for j in range(4):
+        ys(batches - 1, j).wait()
+    for r in range(1, steps):
+        out_b(r).wait()
+    little.wait()
+    for copy in swaps:
+        copy.wait()
+
+
+def expert(x, ct_rows, wi, wb, bi, bb, idx, probs, hid, ct, small, n, half):
+    slots = x.shape[1]
+    rows = n * slots
+    hidden = wi[0].shape[1]
     experts, lanes = probs.shape
     tr = up(ct.shape[0], 16)
     chunks = len(row_chunks(tr))
+    shape = jax.ShapeDtypeStruct
     sem = pltpu.SemaphoreType.DMA
+    vmem = pltpu.VMEM
+    far = pl.BlockSpec(memory_space=pl.ANY)
     return pl.pallas_call(
-        functools.partial(return_kernel, n, half),
+        functools.partial(expert_kernel, n, half, experts),
         out_shape=(
-            jax.ShapeDtypeStruct(ct.shape, F32),
-            jax.ShapeDtypeStruct((128, D), F32),
+            shape(ct.shape, F32), shape((up(experts + 3, 8), D), F32), shape((n, slots, D), BF),
+            shape((D, hidden), F32), shape((D, hidden), BF),
+            shape((hidden, D), F32), shape((hidden, D), BF),
+            shape((8, 2 * hidden + D), F32), shape((8, 2 * hidden + D), F32),
         ),
-        in_specs=[whole()] * 7,
-        out_specs=(whole(),) * 2,
+        in_specs=[whole(), far, far, far, far, far, whole(), whole(), whole(),
+                  whole(), whole(), far, whole(), whole()],
+        out_specs=(whole(), whole(), far, far, far, far, far, whole(), whole()),
         scratch_shapes=[
-            pltpu.VMEM((n, slots, D), BF),
-            pltpu.VMEM((lanes, D), F32),
-            pltpu.VMEM((tr, D), BF),
-            pltpu.VMEM((tr, D), BF),
-            pltpu.VMEM((2 * experts, lanes), F32),
-            pltpu.VMEM((2 * experts, lanes), F32),
-            sem((n,)), sem((n,)), sem((chunks + 1,)), sem((chunks + 1,)),
+            vmem((D, hidden), BF), vmem((D, hidden), BF), vmem((hidden, D), BF), vmem((hidden, D), BF),
+            vmem((rows, D), BF),
+            vmem((rows, hidden), BF), vmem((rows, hidden), BF),
+            vmem((rows, hidden), BF), vmem((rows, hidden), BF),
+            vmem((n, slots, D), BF), vmem((n, slots, D), BF),
+            vmem((lanes, D), F32), vmem((tr, D), BF),
+            vmem((4, slots, D), BF), vmem((4, slots, D), BF),
+            vmem((2, hidden // 3, D), F32),
+            vmem((experts, lanes), F32), vmem((experts, lanes), F32),
+            sem((5,)), sem((2, 4)), sem((3, 3)), sem((n,)), sem((n,)),
+            sem((chunks + 1,)), sem((chunks + 1,)), sem((3,)), sem((3,)),
         ],
         compiler_params=params(collective_id=2, has_side_effects=True),
-        name="give_back",
-    )(dx, idx, probs, n2, hid, ct, small)
+        name="expert",
+    )(x, ct_rows, wi[0], wi[1], wb[0], wb[1], bi[0], bi[1], bb, idx, probs, hid, ct, small)
 
 
 def attend_back_kernel(
-    experts, hg_ref, tok_ref, small_ref, w_ref, qkv_ref, att_ref, dn_ref, dw_ref,
+    experts, hg_ref, tok_ref, small_ref, w_ref, qkv_ref, att_ref, gi_ref, gi_in, gb_ref, gb_in, little_ref, little_in,
+    dn_ref, dw_ref, gi_out, gb_out, gbi_out, gbb_out,
     normed, low, dqkv, pp,
 ):
     images = normed.shape[0]
     scale = HD ** (-0.5)
-    gains = jnp.transpose(small_ref[...].astype(F32))
-    gain = gains[experts : experts + 1, :]
-    tail = jnp.zeros((images, 16, D), F32)
-    pp[:, SEQ_PAD - 16 : SEQ_PAD, :] = tail
-    for i in range(images):
-        pp[i, 0:SEQ, :] = hg_ref[i * SEQ : (i + 1) * SEQ, :]
-    low[...] = pp[...].astype(BF)
-    for i in range(images):
-        pp[i, 0:SEQ, :] = tok_ref[i * SEQ : (i + 1) * SEQ, :].astype(F32)
-    lane = lax.broadcasted_iota(jnp.int32, (1, 2 * HD), 1)
-    masks = [jnp.where(lane // HD == h, 1.0, 0.0).astype(BF) for h in range(2)]
-    valid = lax.broadcasted_iota(jnp.int32, (1, SEQ_PAD), 1) < SEQ
-
-    def image(i, carry):
+    step = pl.program_id(0)
+    gi_out[...] = gi_ref[...] + gi_in[...].astype(F32)
+    gb_out[...] = gb_ref[...] + gb_in[...].astype(F32)
+
+    @pl.when(step == 0)
+    def _():
+        hidden = gbi_out.shape[1]
+        gbi_out[...] = little_ref[0:1, 0:hidden] + little_in[0:1, hidden : 2 * hidden]
+        gbb_out[...] = little_ref[0:1, 2 * hidden :] + little_in[0:1, 2 * hidden :]
+        pp[:, SEQ_PAD - 16 : SEQ_PAD, :] = jnp.zeros((images, 16, D), F32)
+        for i in range(images):
+            pp[i, 0:SEQ, :] = hg_ref[i * SEQ : (i + 1) * SEQ, :]
+        low[...] = pp[...].astype(BF)
+        for i in range(images):
+            pp[i, 0:SEQ, :] = tok_ref[i * SEQ : (i + 1) * SEQ, :].astype(F32)
+
+    @pl.when(step < images)
+    def _():
+        i = step
+        gains = jnp.transpose(small_ref[...].astype(F32))
+        gain = gains[experts : experts + 1, :]
+        lane = lax.broadcasted_iota(jnp.int32, (1, 2 * HD), 1)
+        masks = [jnp.where(lane // HD == h, 1.0, 0.0).astype(BF) for h in range(2)]
+        valid = lax.broadcasted_iota(jnp.int32, (1, SEQ_PAD), 1) < SEQ
         xhat, _ = norm_rows(pp[i])
         normed[i] = (xhat * gain).astype(BF)
         grad_att = mm(low[i], w_ref[3], 1, 0).astype(BF)
@@ -703,45 +695,54 @@
         for c in range(1, 3):
             total += mm(dqkv[c, i], w_ref[c], 1, 1)
         pp[i] = total
-        return carry
-
-    lax.fori_loop(0, images, image, 0)
-    for i in range(images):
-        dn_ref[i * SEQ : (i + 1) * SEQ, :] = pp[i, 0:SEQ, :]
-    rows = images * SEQ_PAD
-
-    def weight(r, carry):
-        at = pl.ds(pl.multiple_of(r * 256, 256), 256)
-        left = normed[:, :, at].reshape(rows, 256)
-        for c in range(3):
-            dw_ref[c, at, :] = mm(left, dqkv[c].reshape(rows, -1), 0, 0).astype(BF)
-        left = low[:, :, at].reshape(rows, 256)
-        dw_ref[3, at, :] = mm(left, att_ref[...].reshape(rows, -1), 0, 0).astype(BF)
-        return carry
-
-    lax.fori_loop(0, D // 256, weight, 0)
-
-
-def attend_back(hg, tok, small, w, qkv, att, experts):
+
+    @pl.when(step == images)
+    def _():
+        for i in range(images):
+            dn_ref[i * SEQ : (i + 1) * SEQ, :] = pp[i, 0:SEQ, :]
+        rows = images * SEQ_PAD
+
+        def weight(r, carry):
+            at = pl.ds(pl.multiple_of(r * 256, 256), 256)
+            left = normed[:, :, at].reshape(rows, 256)
+            for c in range(3):
+                dw_ref[c, at, :] = mm(left, dqkv[c].reshape(rows, -1), 0, 0).astype(BF)
+            left = low[:, :, at].reshape(rows, 256)
+            dw_ref[3, at, :] = mm(left, att_ref[...].reshape(rows, -1), 0, 0).astype(BF)
+            return carry
+
+        lax.fori_loop(0, D // 256, weight, 0)
+
+
+def attend_back(hg, tok, small, w, qkv, att, gi, gi_in, gb, gb_in, little, little_in, experts):
     images = tok.shape[0] // SEQ
     width = w.shape[2]
+    steps = images + 1
+    hidden = gi.shape[1]
+    line_i = pl.BlockSpec((gi.shape[0] // steps, hidden), lambda k: (k, 0))
+    line_b = pl.BlockSpec((hidden // steps, D), lambda k: (k, 0))
     return pl.pallas_call(
         functools.partial(attend_back_kernel, experts),
+        grid=(steps,),
         out_shape=(
             jax.ShapeDtypeStruct(tok.shape, F32),
             jax.ShapeDtypeStruct((4, D, width), BF),
+            jax.ShapeDtypeStruct(gi.shape, F32),
+            jax.ShapeDtypeStruct(gb.shape, F32),
+            jax.ShapeDtypeStruct((1, hidden), F32),
+            jax.ShapeDtypeStruct((1, D), F32),
         ),
-        in_specs=[whole()] * 6,
-        out_specs=(whole(),) * 2,
+        in_specs=[whole()] * 6 + [line_i, line_i, line_b, line_b, whole(), whole()],
+        out_specs=(whole(), whole(), line_i, line_b, whole(), whole()),
         scratch_shapes=[
             pltpu.VMEM((images, SEQ_PAD, D), BF),
             pltpu.VMEM((images, SEQ_PAD, D), BF),
             pltpu.VMEM((3, images, SEQ_PAD, width), BF),
             pltpu.VMEM((images, SEQ_PAD, D), F32),
         ],
-        compiler_params=params(),
+        compiler_params=params(dimension_semantics=("arbitrary",)),
         name="attend_back",
-    )(hg, tok, small, w, qkv, att)
+    )(hg, tok, small, w, qkv, att, gi, gi_in, gb, gb_in, little, little_in)
 
 
 def last_kernel(
@@ -784,6 +785,7 @@
         gain_sum += jnp.sum(grad * xhat, axis=0, keepdims=True)
     row = lax.broadcasted_iota(jnp.int32, sg_ref.shape, 0)
     rows = jnp.where(row == experts + 2, gain_sum, sg_ref[...])
+    rows = jnp.concatenate([rows, jnp.zeros((128 - rows.shape[0], D), F32)], axis=0)
     turned = jnp.transpose(rows).astype(BF)
     real = turned.shape[0] // n
     for b in range(n):
@@ -927,18 +929,13 @@
 
     qkv, att, part = attend(tokens, small, weights, experts)
     hid, n2, probs, x = dispatch(part, tokens, small, idx, n, experts, half, slots)
-    rows = n * slots
-    gi_own, gi_sib, gb_own, gb_sib, gbi_own, gbi_sib, gbb, dx, y = expert(
-        x.reshape(rows, D), ct_rows.reshape(rows, D), wi, wb, bi, back_bias, n, half, slots
+    hg, sg, y, gi, gi_in, gb, gb_in, little, little_in = expert(
+        x, ct_rows, wi, wb, bi, back_bias, idx, probs, hid, cotangent, small, n, half
     )
-    y = lax.all_to_all(y.reshape(n, slots, D), "dp", split_axis=0, concat_axis=0, tiled=True)
-    gi_sib = lax.ppermute(gi_sib, "mp", swap)
-    gb_sib = lax.ppermute(gb_sib, "mp", swap)
-    little = jnp.concatenate([gbi_sib, gbb], axis=1)
-    little = lax.ppermute(little, "mp", swap)
-    hidden = gbi_own.shape[1]
-    hg, sg = give_back(dx.reshape(n, slots, D), idx, probs, n2, hid, cotangent, small, n, half)
-    dn, dw = attend_back(hg, tokens, small, weights, qkv, att, experts)
+    y = lax.all_to_all(y, "dp", split_axis=0, concat_axis=0, tiled=True)
+    dn, dw, gi, gb, gbi, gbb = attend_back(
+        hg, tokens, small, weights, qkv, att, gi, gi_in, gb, gb_in, little, little_in, experts
+    )
     dw = dw.reshape(4, n, shard, width)
     if rp > shard:
         dw = jnp.pad(dw, ((0, 0), (0, 0), (0, rp - shard), (0, 0)))
@@ -953,10 +950,10 @@
         gs[:, experts + 1],
         gs[:, experts],
         gs[:, :experts],
-        (gi_own + gi_sib.astype(F32))[None],
-        gbi_own + little[:, :hidden],
-        (gb_own + gb_sib.astype(F32))[None],
-        gbb + little[:, hidden:],
+        gi[None],
+        gbi,
+        gb[None],
+        gbb,
     )
 
 

time: 431 us -> 348 us (0.81)
  Pallas kernels: 373 us -> 300 us
  other arithmetic: 13.5 us -> 1.6 us
  starting transfers between devices: 21.4 us -> 13.3 us
  waiting for transfers between devices: 0.02 us -> 7.92 us
    pallas_call x3 -> x2, Pallas kernels: 191 us -> 121 us  [the longest x1 85.2 us: expert(): pl.pallas_call(functools.partial(expert_kernel, n, half, experts), out_sh...]
    broadcast_in_dim x2 -> x0, other arithmetic: 10.7 us -> none  [the longest x1 6.14 us: body(): (gi_own + gi_sib.astype(F32))[None]]
    all_to_all x1, waiting for transfers between devices: 0.01 us -> 7.91 us  [body(): y = lax.all_to_all(y, 'dp', split_axis=0, concat_axis=0, tiled=True)]
    all_to_all x1, starting transfers between devices: 9.1 us -> 4.56 us  [body(): y = lax.all_to_all(y, 'dp', split_axis=0, concat_axis=0, tiled=True)]
  transfers between devices with their start and end apart: 8 -> 5, of which waited for: 0 -> 1; matrix products, arithmetic and copies ran while one was open for 3% -> 0% of each run, Pallas kernels for 49% -> 34%
where the time goes in v2:
time: 348 us; the launch traced here: 343 us
  Pallas kernels  300 us (86%)
  local copies, waits for them, and re-layouts  19.3 us (6%)
  starting transfers between devices  13.3 us (4%)
  waiting for transfers between devices  7.92 us (2%)
    pallas_call x1, Pallas kernels, expert(): pl.pallas_call(functools.partial(expert_kernel, n, half, experts), out_sh...  85.2 us
    pallas_call x1, Pallas kernels, dispatch(): pl.pallas_call(functools.partial(dispatch_kernel, n, half), out_shape=(ja...  67.8 us
    pallas_call x1, Pallas kernels, last(): pl.pallas_call(functools.partial(last_kernel, n, experts), out_shape=(jax...  55.7 us
    pallas_call x1, Pallas kernels, attend_back(): pl.pallas_call(functools.partial(attend_back_kernel, experts), grid=(step...  35.6 us
    pallas_call x1, Pallas kernels, gather_weights(): pl.pallas_call(functools.partial(gather_kernel, n), out_shape=(jax.ShapeD...  34.3 us
    pallas_call x1, Pallas kernels, attend(): pl.pallas_call(functools.partial(attend_kernel, experts), out_shape=(jax....  14.5 us
    unnamed x16, local copies, waits for them, and re-layouts  8.48 us
    all_to_all x1, waiting for transfers between devices, body(): y = lax.all_to_all(y, 'dp', split_axis=0, concat_axis=0, tiled=True)  7.91 us
  transfers between devices with their start and end apart: 5, of which 1 were waited for; matrix products, arithmetic and copies ran while one was open for 0% of the time, Pallas kernels for 34%

profile of v2, /device:TPU:9, one launch (start us, length us, event | category | flops | bytes accessed | tf_op | source)
XLA Modules:
  0.0 343.1 jit_solution(11293925875209523708)
XLA Ops:
  1.4 0.8 copy.35
  2.2 0.8 copy.34
  2.9 0.8 copy.32
  4.4 1.0 copy.31.pcol_ref
  5.4 1.3 pad.9.rt_ref
  6.7 1.6 pad_maximum_fusion.w_ref
  9.0 34.3 %gather_weights.1 = (bf16[4,768,384]{2,1,0:T(8,128)(2,1)}, bf16[768,128]{1,0:T(8,128)(2,1)}) custom-call(bf16[4,48,384]{2,1,0:T(8,128)(2,1)} %pad_maximum_fusion.w_ref, bf16[48,128]{1,0:T(8,128)(2,1)} %concatenate.7.s_ref), custom_call_target="tpu_custom_call" | custom-call | tf_op jit(solution)/shard_map/gather_weights/pallas_call | solution.py:181
  43.3 6.8 %route.1 = (s32[2,1024]{1,0:T(2,128)}, bf16[16,80,768]{2,1,0:T(8,128)(2,1)}) custom-call(s32[1,1024]{1,0:T(1,128)} %bitcast.31, s32[1024,1]{1,0:T(8,128)} %copy.31.pcol_ref, s32[2,1024]{1,0:T(2,128)} %pad.9.rt_ref, bf16[985,768]{1,0:T(8,128)(2,1)} %tok_ct.1), custom_call_target="tpu_custom_call" | custom-call | tf_op jit(solution)/shard_map/route/pallas_call | solution.py:115
  50.1 5.5 %all-to-all-start = ((bf16[16,80,768]{2,1,0:T(8,128)(2,1)}), bf16[16,80,768]{2,1,0:T(8,128)(2,1)S(1)}, u32[]{:S(2)}, u32[]{:S(2)}) async-start(bf16[16,80,768]{2,1,0:T(8,128)(2,1)} %get-tuple-element.50), calls=%async_computation | async-start | bytes 3932160 | tf_op jit(solution)/shard_map/all_to_all | solution.py:928
  55.6 2.8 collective-permute-start
  58.9 14.5 %attend.1 = (bf16[3,5,208,384]{3,2,1,0:T(8,128)(2,1)}, bf16[5,208,384]{2,1,0:T(8,128)(2,1)}, f32[985,768]{1,0:T(8,128)}) custom-call(bf16[985,768]{1,0:T(8,128)(2,1)} %tok_ref.7, bf16[768,128]{1,0:T(8,128)(2,1)} %get-tuple-element.45.small_ref, bf16[4,768,384]{2,1,0:T(8,128)(2,1)} %get-tuple-element.46.w_ref), custom_call_target="tpu_custom_call" | custom-call | tf_op jit(solution)/shard_map/attend/pallas_call | solution.py:237
  73.4 67.8 %dispatch.1 = (f32[985,768]{1,0:T(8,128)}, bf16[1024,768]{1,0:T(8,128)(2,1)}, f32[16,1024]{1,0:T(8,128)}, bf16[16,80,768]{2,1,0:T(8,128)(2,1)}) custom-call(f32[985,768]{1,0:T(8,128)} %get-tuple-element.47.part_ref, bf16[985,768]{1,0:T(8,128)(2,1)} %tok_ref.7, bf16[768,128]{1,0:T(8,128)(2,1)} %get-tuple-element.45.small_ref, s32[2,1024]{1,0:T(2,128)} %get-tuple-element.48.idx_ref), custom_call_target="tpu_custom_call" | custom-call | tf_op jit(solution)/shard_map/dispatch/pallas_call | solution.py:338
  142.6 85.2 %expert.1 = (f32[985,768]{1,0:T(8,128)}, f32[24,768]{1,0:T(8,128)}, bf16[16,80,768]{2,1,0:T(8,128)(2,1)}, f32[768,1536]{1,0:T(8,128)}, bf16[768,1536]{1,0:T(8,12...) custom-call(bf16[16,80,768]{2,1,0:T(8,128)(2,1)} %get-tuple-element.49.x_ref, ...), custom_call_target="tpu_custom_call" | custom-call | tf_op jit(solution)/shard_map/expert/pallas_call | solution.py:609
  227.8 4.6 %all-to-all-start.1 = ((bf16[16,80,768]{2,1,0:T(8,128)(2,1)}), bf16[16,80,768]{2,1,0:T(8,128)(2,1)S(1)}, u32[]{:S(2)}, u32[]{:S(2)}) async-start(bf16[16,80,768]{2,1,0:T(8,128)(2,1)} %get-tuple-element.65), calls=%async_computation.1 | async-start | bytes 3932160 | tf_op jit(solution)/shard_map/all_to_all | solution.py:935
  232.4 35.6 %attend_back.1 = (f32[985,768]{1,0:T(8,128)}, bf16[4,768,384]{2,1,0:T(8,128)(2,1)}, f32[768,1536]{1,0:T(8,128)}, f32[1536,768]{1,0:T(8,128)}, f32[1,1536]{1,0:T(1,128)}, /*index=5*/f32[1,768]{1,0:T(1,128)}) custom-call(f32[985,768]{1,0:T(8,128)} %get-tuple-element.53.hg_ref, bf16[985,768]{1,0:T(8,128)(2,1)} %tok_ref.7, ...), custom_call_target="tpu_custom_call" | custom-call | tf_op jit(solution)/shard_map/attend_back/pallas_call | solution.py:724
  268.0 7.9 %all-to-all-done.1.y_ref = bf16[16,80,768]{2,1,0:T(8,128)(2,1)S(1)} async-done(((bf16[16,80,768]{2,1,0:T(8,128)(2,1)}), bf16[16,80,768]{2,1,0:T(8,128)(2,1)S(1)}, u32[]{:S(2)}, u32[]{:S(2)}) %all-to-all-start.1) | async-done | bytes 1966112 | tf_op jit(solution)/shard_map/all_to_all | solution.py:935
  275.9 1.3 copy-done
  277.2 55.7 %last.1 = (bf16[985,768]{1,0:T(8,128)(2,1)}, bf16[985,768]{1,0:T(8,128)(2,1)}, f32[4,48,384]{2,1,0:T(8,128)}, f32[48,128]{1,0:T(8,128)}) custom-call(bf16[4,4,4,48,384]{4,3,2,1,0:T(8,128)(2,1)} %bitcast.27, f32[24,768]{1,0:T(8,128)} %get-tuple-element.63.sg_ref, f32[985,768]{1,0:T(8,128)} %get-tuple-element.64.dn_ref, bf16[985,768]{1,0:T(8,128)(2,1)} %tok_ref.7, ...), custom_call_target="tpu_custom_call" | custom-call | tf_op jit(solution)/shard_map/last/pallas_call | solution.py:863
  332.9 1.6 slice_bitcast_fusion.1
  334.6 1.6 slice_bitcast_fusion
  336.2 1.6 slice_reduce_fusion
  337.8 1.4 copy.36
  339.2 2.6 copy.39
  341.8 1.1 copy.40
  (21 shorter events, 4.0 us)
Async XLA Ops:
  4.4 38.9 %copy-start.3 = (s32[1024]{0:T(1024)}, s32[1024]{0:T(1024)S(1)}, u32[]{:S(2)}) copy-start(s32[1024]{0:T(1024)S(1)} %pad.8) | copy-start | bytes 12292
  50.1 8.4 %copy-start.4 = (bf16[1,1536]{1,0:T(2,128)(2,1)S(1)}, bf16[1,1536]{1,0:T(2,128)(2,1)}, u32[]{:S(2)}) copy-start(bf16[1,1536]{1,0:T(2,128)(2,1)} %bi_own.1) | copy-start | bytes 9220
  50.1 91.2 %all-to-all-start = ((bf16[16,80,768]{2,1,0:T(8,128)(2,1)}), bf16[16,80,768]{2,1,0:T(8,128)(2,1)S(1)}, u32[]{:S(2)}, u32[]{:S(2)}) async-start(bf16[16,80,768]{2,1,0:T(8,128)(2,1)} %get-tuple-element.50), calls=%async_computation | async-start | bytes 3932160 | tf_op jit(solution)/shard_map/all_to_all | solution.py:928
  55.6 85.6 %collective-permute-start = (bf16[768,1536]{1,0:T(8,128)(2,1)}, bf16[768,1536]{1,0:T(8,128)(2,1)}, u32[]{:S(2)}, u32[]{:S(2)}) collective-permute-start(bf16[768,1536]{1,0:T(8,128)(2,1)} %bitcast.23), channel_id=1, source_target_pairs={{0,1},{1,0},{2,3},{3,2},{4,5},{5,4},{6,7},{7,6},{8,9},{9,8},{10,11... | collective-permute-start | bytes 7077896 | tf_op jit(solution)/shard_map/ppermute | solution.py:906
  58.4 82.9 %collective-permute-start.1 = (bf16[1536,768]{1,0:T(8,128)(2,1)}, bf16[1536,768]{1,0:T(8,128)(2,1)}, u32[]{:S(2)}, u32[]{:S(2)}) collective-permute-start(bf16[1536,768]{1,0:T(8,128)(2,1)} %bitcast.25), channel_id=1, source_target_pairs={{0,1},{1,0},{2,3},{3,2},{4,5},{5,4},{6,7},{7,6},{8,9},{9,8},{10,11... | collective-permute-start | bytes 7077896 | tf_op jit(solution)/shard_map/ppermute | solution.py:907
  58.5 82.8 %collective-permute-start.2 = (bf16[1,1536]{1,0:T(2,128)(2,1)S(1)}, bf16[1,1536]{1,0:T(2,128)(2,1)S(1)}, u32[]{:S(2)}, u32[]{:S(2)}) collective-permute-start(bf16[1,1536]{1,0:T(2,128)(2,1)S(1)} %copy-done.4), channel_id=1, source_target_pairs={{0,1},{1,0},{2,3},{3,2},{4,5},{5,4},{6,7},{7,6},{8,9},{9,8},{10,11... | collective-permute-start | bytes 9224 | tf_op jit(solution)/shard_map/ppermute | solution.py:908
  141.2 0.6 copy-start.5
  141.3 1.3 copy-start.1
  227.8 48.1 %all-to-all-start.1 = ((bf16[16,80,768]{2,1,0:T(8,128)(2,1)}), bf16[16,80,768]{2,1,0:T(8,128)(2,1)S(1)}, u32[]{:S(2)}, u32[]{:S(2)}) async-start(bf16[16,80,768]{2,1,0:T(8,128)(2,1)} %get-tuple-element.65), calls=%async_computation.1 | async-start | bytes 3932160 | tf_op jit(solution)/shard_map/all_to_all | solution.py:935
  275.9 1.3 copy-start
  332.9 8.9 %copy-start.2 = (bf16[985,768]{1,0:T(8,128)(2,1)S(1)}, bf16[985,768]{1,0:T(8,128)(2,1)}, u32[]{:S(2)}) copy-start(bf16[985,768]{1,0:T(8,128)(2,1)} %get-tuple-element.114) | copy-start | bytes 4538884

commit v3 on v2

--- a/solution.py
+++ b/solution.py
@@ -75,200 +75,242 @@
     )
 
 
+def partner(me, n, place, sign=1):
+    plane = n // LINE
+    groups = plane // 4
+    z, q = me // plane, me % plane
+    step, j = place // 4, place % 4
+    turn, g = step // groups, step % groups
+    k = 2 * (1 - turn % 2) + turn // 2
+    line = (z // 2 + k // 2) % 2 * 2 + (z % 2 + k % 2) % 2
+    return line * plane + (q + plane + sign * (g * 4 + j)) % plane
+
+
 def slot_matrix(idx_ref, first, rows):
     number = lax.broadcasted_iota(jnp.int32, (rows, idx_ref.shape[1]), 0) + first
     hit = (number == idx_ref[0:1, :]) | (number == idx_ref[1:2, :])
     return jnp.where(hit, 1.0, 0.0).astype(BF)
 
 
-def route_kernel(experts, cap, half, slots, prow_ref, pcol_ref, rt_ref, ct_ref, idx_ref, out_ref, ctp):
-    lanes = rt_ref.shape[1]
-    tok = ct_ref.shape[0]
-    mine = lax.axis_index("mp")
-    ctp[...] = jnp.zeros_like(ctp)
-    ctp[0:tok, :] = ct_ref[...]
+def begin_kernel(
+    n, cap, half, slots,
+    wq_ref, wout_ref, rows_ref, gain_refs, rt_ref, rank_ref, ct_ref, tok_ref,
+    wo_ref, so_ref, idx_ref, ctx_ref, qkv_ref, att_ref, part_ref,
+    gw, gs, mine_w, mine_s, info, ctp, send, xp, pp,
+    zs, zr, ps, pr, cs, cr, lsem,
+):
+    me, mine = lax.axis_index("dp"), lax.axis_index("mp")
+    plane = n // LINE
+    z, q = me // plane, me % plane
+    experts, shard = rows_ref.shape
+    tok = tok_ref.shape[0]
+    lanes = idx_ref.shape[1]
+    rp = mine_w.shape[1]
+    zpeer = [((z + d) % LINE) * plane + q for d in range(1, LINE)]
+    qpeer = [z * plane + (q + d) % plane for d in range(1, plane)]
+    full_w, full_s = (wo_ref, so_ref) if rp == shard else (gw, gs)
+
+    if rp > shard:
+        mine_w[...] = jnp.zeros_like(mine_w)
+    mine_w[0:3, 0:shard, :] = wq_ref[...]
+    mine_w[3, 0:shard, :] = wout_ref[...]
+    pp[0, 0:128, 0:128] = jnp.zeros((128, 128), F32)
+    pp[0, 0:experts, 0:shard] = rows_ref[...].astype(F32)
+    for k, gain_ref in enumerate(gain_refs):
+        pp[0, experts + k : experts + k + 1, 0:shard] = gain_ref[...].astype(F32)
+    mine_s[...] = jnp.transpose(pp[0, 0:128, 0:128])[0:rp, :].astype(BF)
+    greet([{"dp": (me + d) % n} for d in range(1, n)])
+
+    def at(block):
+        rows = pl.ds(pl.multiple_of(block * rp, rp), rp)
+        return full_w.at[:, rows, :], full_s.at[rows, :]
+
+    own = at(me)
+    sends = []
+    for d, p in enumerate(zpeer):
+        for i, (a, b) in enumerate(zip((mine_w, mine_s), own)):
+            sends.append(remote(a, b, zs.at[d, i], zr.at[d, i], {"dp": p}))
+            sends[-1].start()
+    for d, p in enumerate(qpeer):
+        for i, (a, b) in enumerate(zip((mine_w, mine_s), own)):
+            sends.append(remote(a, b, ps.at[d, 0, i], pr.at[d, 0, i], {"dp": p}))
+            sends[-1].start()
+    here = pl.ds(pl.multiple_of(me * rp, rp), rp)
+    full_w[:, here, :] = mine_w[...]
+    full_s[here, :] = mine_s[...]
+
+    info[0:2, :] = jnp.full((2, lanes), -1, jnp.int32)
+    info[2:3, :] = jnp.full((1, lanes), 1 << 20, jnp.int32)
+    info[0:2, 0:tok] = rt_ref[...]
+    info[2:3, 0:tok] = rank_ref[...]
     number = lax.broadcasted_iota(jnp.int32, (experts, lanes), 0)
-    hot = [jnp.where(number == rt_ref[j : j + 1, :], 1.0, 0.0) for j in range(2)]
-    before = jnp.where(pcol_ref[...] < prow_ref[...], 1.0, 0.0).astype(BF)
+    hot = [jnp.where(number == info[j : j + 1, :], 1.0, 0.0) for j in range(2)]
+    ranks = info[2:3, :].astype(F32)
+    column = jnp.transpose(jnp.broadcast_to(ranks, (128, lanes)))[:, 0:1]
+    before = jnp.where(column < ranks, 1.0, 0.0).astype(BF)
     counts = [mm(h.astype(BF), before, 1, 0) for h in hot]
     counts[1] = counts[1] + jnp.sum(hot[0], axis=1, keepdims=True)
     for j in range(2):
         slot = jnp.sum(counts[j] * hot[j], axis=0, keepdims=True).astype(jnp.int32)
         place = slot - mine * half
-        expert = rt_ref[j : j + 1, :]
-        kept = (slot < cap) & (place >= 0) & (place < half) & (expert >= 0)
-        idx_ref[j : j + 1, :] = jnp.where(kept, expert * slots + place, -1)
-
-    group = 4 * slots
-
-    def step(b, carry):
-        rows = slot_matrix(idx_ref, b * group, group)
-        block = mm(rows, ctp[...], 1, 0).astype(BF)
-        out_ref[pl.ds(b * 4, 4)] = block.reshape(4, slots, D)
+        expert_id = info[j : j + 1, :]
+        kept = (slot < cap) & (place >= 0) & (place < half) & (expert_id >= 0)
+        idx_ref[j : j + 1, :] = jnp.where(kept, expert_id * slots + place, -1)
+    ctp[lanes - 64 : lanes, :] = jnp.zeros((64, D), BF)
+    ctp[0:tok, :] = ct_ref[...]
+
+    def rows_of(b, carry):
+        ones = [slot_matrix(idx_ref, partner(me, n, b * 4 + j) * slots, slots) for j in range(4)]
+        block = mm(jnp.concatenate(ones, axis=0), ctp[...], 1, 0).astype(BF)
+        send[pl.ds(b * 4, 4)] = block.reshape(4, slots, D)
         return carry
 
-    lax.fori_loop(0, experts // 4, step, 0)
-
-
-def route(prow, pcol, rt, ct, experts, cap, half, slots):
-    lanes = rt.shape[1]
-    return pl.pallas_call(
-        functools.partial(route_kernel, experts, cap, half, slots),
-        out_shape=(
-            jax.ShapeDtypeStruct((2, lanes), jnp.int32),
-            jax.ShapeDtypeStruct((experts, slots, D), BF),
-        ),
-        in_specs=[whole()] * 4,
-        out_specs=(whole(), whole()),
-        scratch_shapes=[pltpu.VMEM((lanes, D), BF)],
-        compiler_params=params(),
-        name="route",
-    )(prow, pcol, rt, ct)
-
-
-def gather_kernel(n, w_ref, s_ref, wo_ref, so_ref, lsem, zs, zr, ps, pr):
-    me = lax.axis_index("dp")
-    plane = n // LINE
-    z, q = me // plane, me % plane
-    rp = w_ref.shape[1]
-    zpeer = [((z + d) % LINE) * plane + q for d in range(1, LINE)]
-    qpeer = [z * plane + (q + d) % plane for d in range(1, plane)]
-    greet([{"dp": p} for p in zpeer + qpeer])
-
-    def at(block):
-        rows = pl.ds(pl.multiple_of(block * rp, rp), rp)
-        return wo_ref.at[:, rows, :], so_ref.at[rows, :]
-
-    own = at(me)
-    local = [pltpu.make_async_copy(a, b, lsem.at[i]) for i, (a, b) in enumerate(zip((w_ref, s_ref), own))]
-    for c in local:
-        c.start()
-    sends = []
-    for d, p in enumerate(zpeer):
-        for i, (a, b) in enumerate(zip((w_ref, s_ref), own)):
-            c = remote(a, b, zs.at[d, i], zr.at[d, i], {"dp": p})
-            c.start()
-            sends.append(c)
-    for d, p in enumerate(qpeer):
-        for i, (a, b) in enumerate(zip((w_ref, s_ref), own)):
-            c = remote(a, b, ps.at[d, 0, i], pr.at[d, 0, i], {"dp": p})
-            c.start()
-            sends.append(c)
+    lax.fori_loop(0, n // 4, rows_of, 0)
+
     for k in range(1, LINE):
         block = at(((z + LINE - k) % LINE) * plane + q)
         for i in range(2):
             remote(block[i], block[i], zs.at[k - 1, i], zr.at[k - 1, i], {"dp": zpeer[0]}).wait_recv()
         for d, p in enumerate(qpeer):
             for i in range(2):
-                c = remote(block[i], block[i], ps.at[d, k, i], pr.at[d, k, i], {"dp": p})
-                c.start()
-                sends.append(c)
+                sends.append(remote(block[i], block[i], ps.at[d, k, i], pr.at[d, k, i], {"dp": p}))
+                sends[-1].start()
+
+    local = pltpu.make_async_copy(send.at[plane], ctx_ref.at[plane], lsem.at[0])
+    local.start()
+
+    def ship(p, carry):
+        @pl.when(p != plane)
+        def _():
+            remote(send.at[p], ctx_ref.at[p], cs.at[p], cr.at[p], {"dp": partner(me, n, p)}).start()
+
+        return carry
+
+    lax.fori_loop(0, n, ship, 0)
+
+    images = xp.shape[0]
+    scale = HD ** (-0.5)
+    xp[:, SEQ_PAD - 16 : SEQ_PAD, :] = jnp.zeros((images, 16, D), F32)
+    for i in range(images):
+        xp[i, 0:SEQ, :] = tok_ref[i * SEQ : (i + 1) * SEQ, :].astype(F32)
+
+    def norm(i, carry):
+        xhat, _ = norm_rows(xp[i])
+        xp[i] = xhat
+        return carry
+
+    lax.fori_loop(0, images, norm, 0)
     for d in range(1, plane):
         for k in range(LINE):
             block = at(((z + LINE - k) % LINE) * plane + (q + plane - d) % plane)
             for i in range(2):
                 remote(block[i], block[i], ps.at[d - 1, k, i], pr.at[d - 1, k, i], {"dp": qpeer[0]}).wait_recv()
-    for c in sends:
-        c.wait_send()
-    for c in local:
-        c.wait()
-
-
-def gather_weights(w, s, n):
-    parts, rp, width = w.shape
-    plane = n // LINE
-    sem = pltpu.SemaphoreType.DMA
-    return pl.pallas_call(
-        functools.partial(gather_kernel, n),
-        out_shape=(
-            jax.ShapeDtypeStruct((parts, n * rp, width), BF),
-            jax.ShapeDtypeStruct((n * rp, s.shape[1]), BF),
-        ),
-        in_specs=[whole()] * 2,
-        out_specs=(whole(), whole()),
-        scratch_shapes=[
-            sem((2,)), sem((LINE - 1, 2)), sem((LINE - 1, 2)),
-            sem((plane - 1, LINE, 2)), sem((plane - 1, LINE, 2)),
-        ],
-        compiler_params=params(collective_id=0, has_side_effects=True),
-        name="gather_weights",
-    )(w, s)
-
-
-def attend_kernel(experts, tok_ref, small_ref, w_ref, qkv_ref, att_ref, part_ref, xp, pp):
-    images = xp.shape[0]
-    scale = HD ** (-0.5)
-    gains = jnp.transpose(small_ref[...].astype(F32))
-    gain = gains[experts : experts + 1, :]
-    xp[:, SEQ_PAD - 16 : SEQ_PAD, :] = jnp.zeros((images, 16, D), F32)
-    for i in range(images):
-        xp[i, 0:SEQ, :] = tok_ref[i * SEQ : (i + 1) * SEQ, :].astype(F32)
+    if rp > shard:
+        line = lax.broadcasted_iota(jnp.int32, (D, n * rp), 0)
+        where = lax.broadcasted_iota(jnp.int32, (D, n * rp), 1)
+        squeeze = jnp.where(where == line // shard * rp + line % shard, 1.0, 0.0).astype(BF)
+        for c in range(4):
+            wo_ref[c] = mm(squeeze, gw[c], 1, 0).astype(BF)
+        so_ref[...] = mm(squeeze, gs[...], 1, 0).astype(BF)
+    gain = jnp.transpose(so_ref[...].astype(F32))[experts : experts + 1, :]
     lane = lax.broadcasted_iota(jnp.int32, (1, 2 * HD), 1)
     masks = [jnp.where(lane // HD == h, 1.0, 0.0).astype(BF) for h in range(2)]
     valid = lax.broadcasted_iota(jnp.int32, (1, SEQ_PAD), 1) < SEQ
 
     def image(i, carry):
-        xhat, _ = norm_rows(xp[i])
-        normed = (xhat * gain).astype(BF)
+        normed = (xp[i] * gain).astype(BF)
         for c in range(3):
-            qkv_ref[c, i] = mm(normed, w_ref[c], 1, 0).astype(BF)
-        for p in range(w_ref.shape[2] // (2 * HD)):
+            qkv_ref[c, i] = mm(normed, wo_ref[c], 1, 0).astype(BF)
+        for p in range(qkv_ref.shape[3] // (2 * HD)):
             cols = slice(p * 2 * HD, (p + 1) * 2 * HD)
-            q, k, v = (qkv_ref[c, i, :, cols] for c in range(3))
+            qs, ks, vs = (qkv_ref[c, i, :, cols] for c in range(3))
             outs = []
             for h in range(2):
-                scores = mm(q * masks[h], k, 1, 1) * scale
+                scores = mm(qs * masks[h], ks, 1, 1) * scale
                 scores = jnp.where(valid, scores, -1e30)
                 raised = jnp.exp(scores - jnp.max(scores, axis=-1, keepdims=True))
                 weights = raised / jnp.sum(raised, axis=-1, keepdims=True)
-                outs.append(mm(weights.astype(BF), v, 1, 0))
+                outs.append(mm(weights.astype(BF), vs, 1, 0))
             att_ref[i, :, cols] = jnp.where(lane < HD, outs[0], outs[1]).astype(BF)
-        pp[i] = mm(att_ref[i], w_ref[3], 1, 1)
+        pp[i] = mm(att_ref[i], wo_ref[3], 1, 1)
         return carry
 
     lax.fori_loop(0, images, image, 0)
     for i in range(images):
         part_ref[i * SEQ : (i + 1) * SEQ, :] = pp[i, 0:SEQ, :]
-
-
-def attend(tok, small, w, experts):
+    for c in sends:
+        c.wait_send()
+
+    def finish(p, carry):
+        @pl.when(p != plane)
+        def _():
+            remote(send.at[p], ctx_ref.at[p], cs.at[p], cr.at[p], {"dp": partner(me, n, p)}).wait()
+
+        return carry
+
+    lax.fori_loop(0, n, finish, 0)
+    local.wait()
+
+
+def begin(wq, wout, rows, gains, rt, rank, ct, tok, n, experts, cap, half, slots):
     images = tok.shape[0] // SEQ
-    width = w.shape[2]
+    shard, width = wout.shape
+    rp = up(shard, 16)
+    lanes = up(tok.shape[0], 128)
+    plane = n // LINE
+    sem = pltpu.SemaphoreType.DMA
+    shape = jax.ShapeDtypeStruct
+    vmem = pltpu.VMEM
+    spare = n * rp if rp > shard else 16
+
+    def kernel(wq_ref, wout_ref, rows_ref, g1, g2, g3, *rest):
+        begin_kernel(n, cap, half, slots, wq_ref, wout_ref, rows_ref, (g1, g2, g3), *rest)
+
     return pl.pallas_call(
-        functools.partial(attend_kernel, experts),
+        kernel,
         out_shape=(
-            jax.ShapeDtypeStruct((3, images, SEQ_PAD, width), BF),
-            jax.ShapeDtypeStruct((images, SEQ_PAD, width), BF),
-            jax.ShapeDtypeStruct(tok.shape, F32),
+            shape((4, D, width), BF), shape((D, 128), BF), shape((2, lanes), jnp.int32),
+            shape((n, slots, D), BF), shape((3, images, SEQ_PAD, width), BF),
+            shape((images, SEQ_PAD, width), BF), shape((up(tok.shape[0], 16), D), F32),
         ),
-        in_specs=[whole()] * 3,
-        out_specs=(whole(),) * 3,
+        in_specs=[whole()] * 10,
+        out_specs=(whole(), whole(), whole(), pl.BlockSpec(memory_space=pl.ANY), whole(), whole(), whole()),
         scratch_shapes=[
-            pltpu.VMEM((images, SEQ_PAD, D), F32),
-            pltpu.VMEM((images, SEQ_PAD, D), F32),
+            vmem((4, spare, width), BF), vmem((spare, 128), BF),
+            vmem((4, rp, width), BF), vmem((rp, 128), BF), vmem((8, lanes), jnp.int32),
+            vmem((lanes, D), BF), vmem((n, slots, D), BF),
+            vmem((images, SEQ_PAD, D), F32), vmem((images, SEQ_PAD, D), F32),
+            sem((LINE - 1, 2)), sem((LINE - 1, 2)),
+            sem((plane - 1, LINE, 2)), sem((plane - 1, LINE, 2)),
+            sem((n,)), sem((n,)), sem((1,)),
         ],
-        compiler_params=params(),
-        name="attend",
-    )(tok, small, w)
+        compiler_params=params(collective_id=0, has_side_effects=True),
+        name="begin",
+    )(wq, wout, rows, *gains, rt, rank, ct, tok)
 
 
 def row_chunks(rows):
     return [(s, min(256, rows - s)) for s in range(0, rows, 256)]
 
 
-def dispatch_kernel(
-    n, half, part_ref, tok_ref, small_ref, idx_ref, hid_ref, n2_ref, prob_ref, x_ref,
-    own, other, send, p2, hs, hr, ss, rs,
+def token_send(n, send, x_ref, xs, xr, p, peer):
+    return remote(send.at[p], x_ref.at[p], xs.at[p], xr.at[p], {"dp": peer})
+
+
+def send_tokens(
+    n, half, early, part_ref, tok_ref, small_ref, idx_ref, hid_ref, n2, prob_ref, x_ref,
+    own, other, send, p2, hs, hr, xs, xr,
 ):
     me, mine = lax.axis_index("dp"), lax.axis_index("mp")
+    plane = n // LINE
     tok = tok_ref.shape[0]
     slots = send.shape[1]
-    experts = prob_ref.shape[0]
+    experts, lanes = prob_ref.shape
+    tr = other.shape[0]
     sibling = {"mp": 1 - mine}
-    greet([sibling] + [{"dp": (me + d) % n} for d in range(1, n)])
-    own[own.shape[0] - 16 :, :] = jnp.zeros((16, D), BF)
+    own[tr - 16 : tr, :] = jnp.zeros((16, D), BF)
     copies = []
-    for c, (start, size) in enumerate(row_chunks(own.shape[0])):
+    for c, (start, size) in enumerate(row_chunks(tr)):
         stop = min(start + size, tok)
         own[start:stop, :] = part_ref[start:stop, :].astype(BF)
         rows = pl.ds(start, size)
@@ -278,16 +320,16 @@
     gains = jnp.transpose(small_ref[...].astype(F32))
     gain = gains[experts + 1 : experts + 2, :]
     bias = gains[experts + 2 : experts + 3, :]
-    n2_ref[n2_ref.shape[0] - 64 :, :] = jnp.zeros((64, D), BF)
-    for c, (start, size) in enumerate(row_chunks(own.shape[0])):
+    n2[lanes - 64 : lanes, 0:D] = jnp.zeros((64, D), BF)
+    for c, (start, size) in enumerate(row_chunks(tr)):
         stop = min(start + size, tok)
         copies[c].wait_recv()
         both = own[start:stop, :].astype(F32) + other[start:stop, :].astype(F32)
         hidden = tok_ref[start:stop, :].astype(F32) + both + bias
         hid_ref[start:stop, :] = hidden
         xhat, _ = norm_rows(hidden)
-        n2_ref[start:stop, :] = (xhat * gain).astype(BF)
-    logits = mm(gains[0:experts, :].astype(BF), n2_ref[...], 1, 1)
+        n2[start:stop, 0:D] = (xhat * gain).astype(BF)
+    logits = mm(gains[0:experts, :].astype(BF), n2[0:lanes, 0:D], 1, 1)
     raised = jnp.exp(logits - jnp.max(logits, axis=0, keepdims=True))
     probs = raised / jnp.sum(raised, axis=0, keepdims=True)
     prob_ref[...] = probs
@@ -298,58 +340,71 @@
     number = lax.broadcasted_iota(jnp.int32, (2 * experts, slots), 0)
 
     def step(b, carry):
-        hot = [slot_matrix(idx_ref, ((me + b * 4 + j) % n) * slots, slots) for j in range(4)]
-        block = mm(jnp.concatenate(hot, axis=0), n2_ref[...], 1, 0)
+        hot = [slot_matrix(idx_ref, partner(me, n, b * 4 + j) * slots, slots) for j in range(4)]
+        block = mm(jnp.concatenate(hot, axis=0), n2[0:lanes, 0:D], 1, 0)
         for j in range(4):
-            d = b * 4 + j
-            peer = (me + d) % n
+            p = b * 4 + j
+            peer = partner(me, n, p)
             gates = mm(p2[...], hot[j], 1, 1)
             row_high = jnp.sum(jnp.where(number == peer, gates, 0.0), axis=0, keepdims=True)
             row_low = jnp.sum(jnp.where(number == peer + experts, gates, 0.0), axis=0, keepdims=True)
             rows = block[j * slots : (j + 1) * slots, :]
             left = jnp.where(place == half, row_high, jnp.where(place == half + 1, row_low, rows[:, 0:slots]))
-            send[d, :, :] = rows.astype(BF)
-            send[d, :, 0:slots] = left.astype(BF)
-
-            @pl.when(d > 0)
+            send[p, :, :] = rows.astype(BF)
+            send[p, :, 0:slots] = left.astype(BF)
+
+            @pl.when((p != plane) & (p < early))
             def _():
-                remote(send.at[d], x_ref.at[d], ss.at[d], rs.at[d], {"dp": peer}).start()
+                token_send(n, send, x_ref, xs, xr, p, peer).start()
 
         return carry
 
     lax.fori_loop(0, n // 4, step, 0)
-    x_ref[0] = send[0]
-
-    def finish(d, carry):
-        source = (me + n - d) % n
-        remote(send.at[d], x_ref.at[d], ss.at[d], rs.at[d], {"dp": source}).wait()
-        return carry
-
-    lax.fori_loop(1, n, finish, 0)
+    x_ref[plane] = send[plane]
     for copy in copies:
         copy.wait_send()
+
+
+def dispatch_kernel(
+    n, half, part_ref, tok_ref, small_ref, idx_ref, hid_ref, prob_ref, x_ref,
+    n2, own, other, send, p2, hs, hr, xs, xr,
+):
+    me, mine = lax.axis_index("dp"), lax.axis_index("mp")
+    plane = n // LINE
+    greet([{"mp": 1 - mine}] + [{"dp": (me + d) % n} for d in range(1, n)])
+    send_tokens(
+        n, half, n, part_ref, tok_ref, small_ref, idx_ref, hid_ref, n2, prob_ref, x_ref,
+        own, other, send, p2, hs, hr, xs, xr,
+    )
+
+    def finish(p, carry):
+        @pl.when(p != plane)
+        def _():
+            token_send(n, send, x_ref, xs, xr, p, partner(me, n, p)).wait()
+
+        return carry
+
+    lax.fori_loop(0, n, finish, 0)
 
 
 def dispatch(part, tok, small, idx, n, experts, half, slots):
     lanes = idx.shape[1]
     tr = up(tok.shape[0], 16)
     sem = pltpu.SemaphoreType.DMA
+    vmem = pltpu.VMEM
     chunks = len(row_chunks(tr))
     return pl.pallas_call(
         functools.partial(dispatch_kernel, n, half),
         out_shape=(
             jax.ShapeDtypeStruct(tok.shape, F32),
-            jax.ShapeDtypeStruct((lanes, D), BF),
             jax.ShapeDtypeStruct((experts, lanes), F32),
             jax.ShapeDtypeStruct((n, slots, D), BF),
         ),
         in_specs=[whole()] * 4,
-        out_specs=(whole(),) * 4,
+        out_specs=(whole(),) * 3,
         scratch_shapes=[
-            pltpu.VMEM((tr, D), BF),
-            pltpu.VMEM((tr, D), BF),
-            pltpu.VMEM((n, slots, D), BF),
-            pltpu.VMEM((2 * experts, lanes), BF),
+            vmem((lanes, D), BF), vmem((tr, D), BF), vmem((tr, D), BF), vmem((n, slots, D), BF),
+            vmem((2 * experts, lanes), BF),
             sem((chunks,)), sem((chunks,)), sem((n,)), sem((n,)),
         ],
         compiler_params=params(collective_id=1, has_side_effects=True),
@@ -358,41 +413,56 @@
 
 
 def expert_kernel(
-    n, half, experts,
-    x_ref, ct_ref, wi_own, wi_sib, wb_own, wb_sib, bi_own, bi_sib, bb_ref,
-    idx_ref, prob_ref, hid_ref, tok_ct, small_ref,
-    hg_ref, sg_ref, y_ref, gi_ref, gi_in, gb_ref, gb_in, little_ref, little_in,
+    n, half, fused,
+    first_ref, ct_ref, wi_own, wi_sib, wb_own, wb_sib, bi_own, bi_sib, bb_ref,
+    idx_ref, seen_ref, tok_ct, small_ref,
+    hg_ref, sg_ref, y_ref, gi_ref, gi_in, gb_ref, gb_in, little_ref, little_in, hid_out, prob_ref,
     vi_own, vi_sib, vb_own, vb_sib, g_s, act_own, act_sib, dp_own, dp_sib, dx_s, back, acc, other,
-    ct_s, y_s, stage, gp, gp_other,
-    lsem, ysem, gsem, ss, rs, hs, hr, ms, mr,
+    ct_s, y_s, stage, gp, gp_other, x_ref, send, p2,
+    lsem, ysem, gsem, ss, rs, hs, hr, ms, mr, xs, xr, es, er,
 ):
     me, mine = lax.axis_index("dp"), lax.axis_index("mp")
     sibling = {"mp": 1 - mine}
+    plane = n // LINE
     slots = x_ref.shape[1]
     tok = tok_ct.shape[0]
+    experts = prob_ref.shape[0]
     hidden = wi_own.shape[1]
     group = 4 * slots
     batches = n // 4
+    tr = other.shape[0]
+    early = n // 2 if fused else n
+    first = (first_ref, acc.at[pl.ds(0, tr), :]) if fused else (first_ref, x_ref)
     loads = [
         pltpu.make_async_copy(a, b, lsem.at[i])
         for i, (a, b) in enumerate(
-            ((wi_own, vi_own), (wb_own, vb_own), (wi_sib, vi_sib), (wb_sib, vb_sib), (hid_ref, hg_ref))
+            (first, (wi_own, vi_own), (wb_own, vb_own), (wi_sib, vi_sib), (wb_sib, vb_sib))
         )
     ]
     for c in loads:
         c.start()
     greet([sibling] + [{"dp": (me + d) % n} for d in range(1, n)])
+    loads[0].wait()
+    if fused:
+        send_tokens(
+            n, half, early, acc, seen_ref, small_ref, idx_ref, hg_ref, act_own, prob_ref, x_ref,
+            g_s, other, send, p2, es, er, xs, xr,
+        )
+        keep = pltpu.make_async_copy(hg_ref, hid_out, lsem.at[5])
+    else:
+        keep = pltpu.make_async_copy(hid_out, hg_ref, lsem.at[5])
+    keep.start()
     little_ref[...] = jnp.zeros_like(little_ref)
 
     def cts(b, j):
-        return pltpu.make_async_copy(ct_ref.at[(me + n - b * 4 - j) % n], ct_s.at[j], ysem.at[0, j])
+        return pltpu.make_async_copy(ct_ref.at[b * 4 + j], ct_s.at[j], ysem.at[0, j])
 
     def ys(b, j):
-        return pltpu.make_async_copy(y_s.at[j], y_ref.at[(me + n - b * 4 - j) % n], ysem.at[1, j])
+        return pltpu.make_async_copy(y_s.at[j], y_ref.at[partner(me, n, b * 4 + j, -1)], ysem.at[1, j])
 
     for j in range(4):
         cts(0, j).start()
-    for c in loads[:4]:
+    for c in loads[1:]:
         c.wait()
     chunk = 768
     row = lax.broadcasted_iota(jnp.int32, (group, 16), 0)
@@ -410,6 +480,22 @@
 
     def batch(b, carry):
         at = pl.ds(pl.multiple_of(b * group, 16), group)
+        if fused:
+            for j in range(4):
+                p = b * 4 + j
+
+                @pl.when(p != plane)
+                def _():
+                    token_send(n, send, x_ref, xs, xr, p, partner(me, n, p)).wait_recv()
+
+            @pl.when(b == batches // 4 - 1)
+            def _():
+                def more(p, carry):
+                    token_send(n, send, x_ref, xs, xr, p, partner(me, n, p)).start()
+                    return carry
+
+                lax.fori_loop(early, n, more, 0)
+
         x = x_ref[pl.ds(b * 4, 4)].reshape(group, D)
         high, low = split_two(mm(pick, x[:, 0:128], 1, 0))
         wide = mm(member, high, 1, 0) + mm(member, low, 1, 0)
@@ -441,11 +527,11 @@
         dx = jnp.concatenate([left, dx[:, 128:]], axis=1)
         dx_s[pl.ds(b * 4, 4)] = dx.astype(BF).reshape(4, slots, D)
         for j in range(4):
-            d = b * 4 + j
-
-            @pl.when(d > 0)
+            p = b * 4 + j
+
+            @pl.when(p != plane)
             def _():
-                remote(dx_s.at[d], back.at[d], ss.at[d], rs.at[d], {"dp": (me + n - d) % n}).start()
+                remote(dx_s.at[p], back.at[p], ss.at[p], rs.at[p], {"dp": partner(me, n, p, -1)}).start()
 
         @pl.when(b > 0)
         def _():
@@ -464,7 +550,7 @@
         return carry
 
     lax.fori_loop(0, batches, batch, 0)
-    back[0] = dx_s[0]
+    back[plane] = dx_s[plane]
     little = remote(little_ref, little_in, ms.at[2], mr.at[2], sibling)
     little.start()
 
@@ -507,9 +593,9 @@
         hot = []
         for j in range(4):
             d = b * 4 + j
-            source = (me + d) % n
-
-            @pl.when(d > 0)
+            source = partner(me, n, d)
+
+            @pl.when(d != plane)
             def _():
                 remote(dx_s.at[d], back.at[d], ss.at[d], rs.at[d], {"dp": source}).wait_recv()
 
@@ -540,6 +626,7 @@
     swaps.append(copy)
     lax.fori_loop(batches // 2, batches, combine, 0)
 
+    little.wait()
     copies = []
     own = g_s
     own[other.shape[0] - 16 : other.shape[0], :] = jnp.zeros((16, D), BF)
@@ -553,7 +640,7 @@
     copy = remote(gp, gp_other, hs.at[len(copies)], hr.at[len(copies)], sibling)
     copy.start()
     copy.wait()
-    probs = prob_ref[...]
+    probs = prob_ref[...] if fused else seen_ref[...]
     grad_probs = gp[...] + gp_other[...]
     logits = (probs * (grad_probs - jnp.sum(grad_probs * probs, axis=0, keepdims=True))).astype(BF)
     gains = jnp.transpose(small_ref[...].astype(F32))
@@ -564,7 +651,7 @@
     bias_sum = jnp.zeros((1, D), F32)
     lanes = acc.shape[0]
     act_own[lanes - 64 : lanes, 0:D] = jnp.zeros((64, D), BF)
-    loads[4].wait()
+    keep.wait()
     for c, (start, length) in enumerate(row_chunks(other.shape[0])):
         stop = min(start + length, tok)
         copies[c].wait_recv()
@@ -581,42 +668,66 @@
     for copy in copies:
         copy.wait_send()
 
-    def finish(d, carry):
-        remote(dx_s.at[d], back.at[d], ss.at[d], rs.at[d], {"dp": (me + n - d) % n}).wait_send()
+    def finish(p, carry):
+        @pl.when(p != plane)
+        def _():
+            remote(dx_s.at[p], back.at[p], ss.at[p], rs.at[p], {"dp": partner(me, n, p, -1)}).wait_send()
+            if fused:
+                token_send(n, send, x_ref, xs, xr, p, partner(me, n, p)).wait_send()
+
         return carry
 
-    lax.fori_loop(1, n, finish, 0)
+    lax.fori_loop(0, n, finish, 0)
     for j in range(4):
         ys(batches - 1, j).wait()
     for r in range(1, steps):
         out_b(r).wait()
-    little.wait()
     for copy in swaps:
         copy.wait()
 
 
-def expert(x, ct_rows, wi, wb, bi, bb, idx, probs, hid, ct, small, n, half):
-    slots = x.shape[1]
+def expert(first, ct_rows, wi, wb, bi, bb, idx, probs, hid, tok, ct, small, n, half):
+    fused = hid is None
+    _, slots, _ = ct_rows.shape
     rows = n * slots
     hidden = wi[0].shape[1]
-    experts, lanes = probs.shape
+    lanes = idx.shape[1]
+    experts = n
     tr = up(ct.shape[0], 16)
     chunks = len(row_chunks(tr))
     shape = jax.ShapeDtypeStruct
     sem = pltpu.SemaphoreType.DMA
     vmem = pltpu.VMEM
     far = pl.BlockSpec(memory_space=pl.ANY)
+    outs = [
+        shape(ct.shape, F32), shape((up(experts + 3, 8), D), F32), shape((n, slots, D), BF),
+        shape((D, hidden), F32), shape((D, hidden), BF),
+        shape((hidden, D), F32), shape((hidden, D), BF),
+        shape((8, 2 * hidden + D), F32), shape((8, 2 * hidden + D), F32),
+    ]
+    out_specs = [whole(), whole(), far, far, far, far, far, whole(), whole()]
+    ins = [first, ct_rows, wi[0], wi[1], wb[0], wb[1], bi[0], bi[1], bb, idx]
+    in_specs = [far, far, far, far, far, far, whole(), whole(), whole(), whole()]
+    if fused:
+        outs += [shape(ct.shape, F32), shape((experts, lanes), F32)]
+        out_specs += [far, whole()]
+        ins += [tok, ct, small]
+        in_specs += [whole()] * 3
+        kernel = functools.partial(expert_kernel, n, half, True)
+    else:
+        ins += [probs, ct, small, hid]
+        in_specs += [whole()] * 3 + [far]
+
+        def kernel(*refs):
+            ins, hid_ref, outs, rest = refs[:13], refs[13], refs[14:23], refs[23:]
+            expert_kernel(n, half, False, *ins, *outs, hid_ref, ins[10], *rest)
+
+    small_x = (n, slots, D) if fused else (1, 16, 128)
     return pl.pallas_call(
-        functools.partial(expert_kernel, n, half, experts),
-        out_shape=(
-            shape(ct.shape, F32), shape((up(experts + 3, 8), D), F32), shape((n, slots, D), BF),
-            shape((D, hidden), F32), shape((D, hidden), BF),
-            shape((hidden, D), F32), shape((hidden, D), BF),
-            shape((8, 2 * hidden + D), F32), shape((8, 2 * hidden + D), F32),
-        ),
-        in_specs=[whole(), far, far, far, far, far, whole(), whole(), whole(),
-                  whole(), whole(), far, whole(), whole()],
-        out_specs=(whole(), whole(), far, far, far, far, far, whole(), whole()),
+        kernel,
+        out_shape=tuple(outs),
+        in_specs=in_specs,
+        out_specs=tuple(out_specs),
         scratch_shapes=[
             vmem((D, hidden), BF), vmem((D, hidden), BF), vmem((hidden, D), BF), vmem((hidden, D), BF),
             vmem((rows, D), BF),
@@ -627,12 +738,14 @@
             vmem((4, slots, D), BF), vmem((4, slots, D), BF),
             vmem((2, hidden // 3, D), F32),
             vmem((experts, lanes), F32), vmem((experts, lanes), F32),
-            sem((5,)), sem((2, 4)), sem((3, 3)), sem((n,)), sem((n,)),
+            vmem((n, slots, D), BF), vmem(small_x, BF), vmem((2 * experts, lanes), BF),
+            sem((6,)), sem((2, 4)), sem((3, 3)), sem((n,)), sem((n,)),
             sem((chunks + 1,)), sem((chunks + 1,)), sem((3,)), sem((3,)),
+            sem((n,)), sem((n,)), sem((chunks,)), sem((chunks,)),
         ],
         compiler_params=params(collective_id=2, has_side_effects=True),
         name="expert",
-    )(x, ct_rows, wi[0], wi[1], wb[0], wb[1], bi[0], bi[1], bb, idx, probs, hid, ct, small)
+    )(*ins)
 
 
 def attend_back_kernel(
@@ -898,7 +1011,6 @@
     cap = max(2, 5 * tok // (2 * experts))
     half = (cap + 1) // 2
     slots = up(half + FREE, 16)
-    lanes = up(tok, 128)
     shard, width = w_qkv.shape[0], w_qkv.shape[2]
     rp = up(shard, 16)
     swap = [(0, 1), (1, 0)]
@@ -907,31 +1019,20 @@
     wb = (w_back[0], lax.ppermute(w_back[0], "mp", swap))
     bi = (in_bias, lax.ppermute(in_bias, "mp", swap))
 
-    rt = jnp.pad(routes.T, ((0, 0), (0, lanes - tok)), constant_values=-1)
-    ranks = jnp.pad(priority[0], (0, lanes - tok), constant_values=1 << 20)
-    idx, ct_rows = route(ranks[None, :], ranks[:, None], rt, cotangent, experts, cap, half, slots)
-
-    weights = jnp.concatenate([jnp.swapaxes(w_qkv, 0, 1), w_out.T[None]], axis=0)
-    small = jnp.concatenate(
-        [router, ln1_gain[:, None], ln2_gain[:, None], out_bias[:, None],
-         jnp.zeros((shard, 128 - experts - 3), BF)], axis=1,
+    weights, small, idx, ct_rows, qkv, att, part = begin(
+        jnp.swapaxes(w_qkv, 0, 1), w_out.T, router.T,
+        (ln1_gain[None], ln2_gain[None], out_bias[None]),
+        routes.T, priority, cotangent, tokens, n, experts, cap, half, slots,
     )
-    if rp > shard:
-        weights = jnp.pad(weights, ((0, 0), (0, rp - shard), (0, 0)))
-        small = jnp.pad(small, ((0, rp - shard), (0, 0)))
-    weights, small = gather_weights(weights, small, n)
-    if rp > shard:
-        weights = weights.reshape(4, n, rp, width)[:, :, :shard].reshape(4, D, width)
-        small = small.reshape(n, rp, 128)[:, :shard].reshape(D, 128)
-
-    ct_rows, small = lax.optimization_barrier((ct_rows, small))
-    ct_rows = lax.all_to_all(ct_rows, "dp", split_axis=0, concat_axis=0, tiled=True)
-
-    qkv, att, part = attend(tokens, small, weights, experts)
-    hid, n2, probs, x = dispatch(part, tokens, small, idx, n, experts, half, slots)
-    hg, sg, y, gi, gi_in, gb, gb_in, little, little_in = expert(
-        x, ct_rows, wi, wb, bi, back_bias, idx, probs, hid, cotangent, small, n, half
-    )
+    if n * slots <= 1536:
+        hg, sg, y, gi, gi_in, gb, gb_in, little, little_in, hid, _ = expert(
+            part, ct_rows, wi, wb, bi, back_bias, idx, None, None, tokens, cotangent, small, n, half
+        )
+    else:
+        hid, probs, x = dispatch(part, tokens, small, idx, n, experts, half, slots)
+        hg, sg, y, gi, gi_in, gb, gb_in, little, little_in = expert(
+            x, ct_rows, wi, wb, bi, back_bias, idx, probs, hid, tokens, cotangent, small, n, half
+        )
     y = lax.all_to_all(y, "dp", split_axis=0, concat_axis=0, tiled=True)
     dn, dw, gi, gb, gbi, gbb = attend_back(
         hg, tokens, small, weights, qkv, att, gi, gi_in, gb, gb_in, little, little_in, experts

time: 348 us -> 315 us (0.905)
  Pallas kernels: 300 us -> 281 us
  local copies, waits for them, and re-layouts: 19.3 us -> 11.9 us
  starting transfers between devices: 13.3 us -> 7.27 us
    pallas_call x5 -> x2, Pallas kernels: 209 us -> 190 us  [the longest x1 122 us: expert(): pl.pallas_call(kernel, out_shape=tuple(outs), in_specs=in_specs, out_spec...]
    all_to_all x1 -> x0, starting transfers between devices: 5.48 us -> none  [body(): lax.all_to_all(ct_rows, 'dp', split_axis=0, concat_axis=0, tiled=True)]
    unnamed x16 -> x9, local copies, waits for them, and re-layouts: 8.48 us -> 7.01 us
  transfers between devices with their start and end apart: 5 -> 4, of which waited for: 1 -> 1; matrix products, arithmetic and copies ran while one was open for 0% -> 0% of each run, Pallas kernels for 34% -> 33%
where the time goes in v3:
time: 315 us; the launch traced here: 309 us
  Pallas kernels  281 us (89%)
  local copies, waits for them, and re-layouts  11.9 us (4%)
  waiting for transfers between devices  7.65 us (2%)
  starting transfers between devices  7.27 us (2%)
    pallas_call x1, Pallas kernels, expert(): pl.pallas_call(kernel, out_shape=tuple(outs), in_specs=in_specs, out_spec...  122 us
    pallas_call x1, Pallas kernels, begin(): pl.pallas_call(kernel, out_shape=(shape((4, D, width), BF), shape((D, 128...  67.5 us
    pallas_call x1, Pallas kernels, last(): pl.pallas_call(functools.partial(last_kernel, n, experts), out_shape=(jax...  55.6 us
    pallas_call x1, Pallas kernels, attend_back(): pl.pallas_call(functools.partial(attend_back_kernel, experts), grid=(step...  35.6 us
    all_to_all x1, waiting for transfers between devices, body(): y = lax.all_to_all(y, 'dp', split_axis=0, concat_axis=0, tiled=True)  7.64 us
    unnamed x9, local copies, waits for them, and re-layouts  7.01 us
  transfers between devices with their start and end apart: 4, of which 1 were waited for; matrix products, arithmetic and copies ran while one was open for 0% of the time, Pallas kernels for 33%

profile of v3, /device:TPU:9, one launch (start us, length us, event | category | flops | bytes accessed | tf_op | source)
XLA Modules:
  0.0 308.8 jit_solution(6971784311171667856)
XLA Ops:
  0.6 0.7 collective-permute-start
  1.4 0.1 collective-permute-start.1
  1.5 0.4 collective-permute-start.2
  1.9 67.5 %begin.1 = (bf16[4,768,384]{2,1,0:T(8,128)(2,1)}, bf16[768,128]{1,0:T(8,128)(2,1)}, s32[2,1024]{1,0:T(2,128)}, bf16[16,80,768]{2,1,0:T(8,128)(2,1)}, bf16[3,5,20...) custom-call(bf16[3,48,384]{2,1,0:T(8,128)(2,1)} %bitcast.25, bf16[48,384]{1,0:T(8,128)(2,1)} %bitcast.26, ...), custom_call_target="tpu_custom_call" | custom-call | tf_op jit(solution)/shard_map/begin/pallas_call | solution.py:269
  69.4 0.0 collective-permute-done.2.bi_sib
  69.4 0.0 copy-start.2
  69.4 0.0 collective-permute-done.wi_sib
  69.4 0.0 collective-permute-done.1.wb_sib
  69.4 0.6 copy-done.2
  70.0 122.1 %expert.1 = (f32[985,768]{1,0:T(8,128)}, f32[24,768]{1,0:T(8,128)}, bf16[16,80,768]{2,1,0:T(8,128)(2,1)}, f32[768,1536]{1,0:T(8,128)}, bf16[768,1536]{1,0:T(8,12...) custom-call(f32[992,768]{1,0:T(8,128)} %get-tuple-element.39.first_r, ...), custom_call_target="tpu_custom_call" | custom-call | tf_op jit(solution)/shard_map/expert/pallas_call | solution.py:726
  192.1 6.0 %all-to-all-start = ((bf16[16,80,768]{2,1,0:T(8,128)(2,1)}), bf16[16,80,768]{2,1,0:T(8,128)(2,1)S(1)}, u32[]{:S(2)}, u32[]{:S(2)}) async-start(bf16[16,80,768]{2,1,0:T(8,128)(2,1)} %get-tuple-element.56), calls=%async_computation | async-start | bytes 3932160 | tf_op jit(solution)/shard_map/all_to_all | solution.py:1036
  198.1 35.6 %attend_back.1 = (f32[985,768]{1,0:T(8,128)}, bf16[4,768,384]{2,1,0:T(8,128)(2,1)}, f32[768,1536]{1,0:T(8,128)}, f32[1536,768]{1,0:T(8,128)}, f32[1,1536]{1,0:T(1,128)}, /*index=5*/f32[1,768]{1,0:T(1,128)}) custom-call(f32[985,768]{1,0:T(8,128)} %get-tuple-element.43.hg_ref, bf16[985,768]{1,0:T(8,128)(2,1)} %tok_ref.3, ...), custom_call_target="tpu_custom_call" | custom-call | tf_op jit(solution)/shard_map/attend_back/pallas_call | solution.py:837
  233.8 7.6 %all-to-all-done.y_ref = bf16[16,80,768]{2,1,0:T(8,128)(2,1)S(1)} async-done(((bf16[16,80,768]{2,1,0:T(8,128)(2,1)}), bf16[16,80,768]{2,1,0:T(8,128)(2,1)S(1)}, u32[]{:S(2)}, u32[]{:S(2)}) %all-to-all-start) | async-done | bytes 1966112 | tf_op jit(solution)/shard_map/all_to_all | solution.py:1036
  241.4 0.0 copy-start
  241.4 1.3 copy-done
  242.7 55.6 %last.1 = (bf16[985,768]{1,0:T(8,128)(2,1)}, bf16[985,768]{1,0:T(8,128)(2,1)}, f32[4,48,384]{2,1,0:T(8,128)}, f32[48,128]{1,0:T(8,128)}) custom-call(bf16[4,4,4,48,384]{4,3,2,1,0:T(8,128)(2,1)} %bitcast.23, f32[24,768]{1,0:T(8,128)} %get-tuple-element.54.sg_ref, f32[985,768]{1,0:T(8,128)} %get-tuple-element.55.dn_ref, bf16[985,768]{1,0:T(8,128)(2,1)} %tok_ref.3, ...), custom_call_target="tpu_custom_call" | custom-call | tf_op jit(solution)/shard_map/last/pallas_call | solution.py:976
  298.3 0.0 copy-start.1
  298.3 1.6 slice_bitcast_fusion.1
  299.9 1.6 slice_bitcast_fusion
  301.6 1.6 slice_reduce_fusion
  303.2 1.4 copy.27
  304.6 2.6 copy.30
  307.2 0.0 copy-done.1
  307.2 1.1 copy.31
Async XLA Ops:
  0.6 68.8 %collective-permute-start = (bf16[768,1536]{1,0:T(8,128)(2,1)}, bf16[768,1536]{1,0:T(8,128)(2,1)}, u32[]{:S(2)}, u32[]{:S(2)}) collective-permute-start(bf16[768,1536]{1,0:T(8,128)(2,1)} %bitcast.19), channel_id=1, source_target_pairs={{0,1},{1,0},{2,3},{3,2},{4,5},{5,4},{6,7},{7,6},{8,9},{9,8},{10,11... | collective-permute-start | bytes 7077896 | tf_op jit(solution)/shard_map/ppermute | solution.py:1018
  1.4 68.0 %collective-permute-start.1 = (bf16[1536,768]{1,0:T(8,128)(2,1)}, bf16[1536,768]{1,0:T(8,128)(2,1)}, u32[]{:S(2)}, u32[]{:S(2)}) collective-permute-start(bf16[1536,768]{1,0:T(8,128)(2,1)} %bitcast.21), channel_id=1, source_target_pairs={{0,1},{1,0},{2,3},{3,2},{4,5},{5,4},{6,7},{7,6},{8,9},{9,8},{10,11... | collective-permute-start | bytes 7077896 | tf_op jit(solution)/shard_map/ppermute | solution.py:1019
  1.5 67.9 %collective-permute-start.2 = (bf16[1,1536]{1,0:T(2,128)(2,1)}, bf16[1,1536]{1,0:T(2,128)(2,1)S(1)}, u32[]{:S(2)}, u32[]{:S(2)}) collective-permute-start(bf16[1,1536]{1,0:T(2,128)(2,1)} %bi_own.1), channel_id=1, source_target_pairs={{0,1},{1,0},{2,3},{3,2},{4,5},{5,4},{6,7},{7,6},{8,9},{9,8},{10,11... | collective-permute-start | bytes 9224 | tf_op jit(solution)/shard_map/ppermute | solution.py:1020
  69.4 0.6 copy-start.2
  192.1 49.3 %all-to-all-start = ((bf16[16,80,768]{2,1,0:T(8,128)(2,1)}), bf16[16,80,768]{2,1,0:T(8,128)(2,1)S(1)}, u32[]{:S(2)}, u32[]{:S(2)}) async-start(bf16[16,80,768]{2,1,0:T(8,128)(2,1)} %get-tuple-element.56), calls=%async_computation | async-start | bytes 3932160 | tf_op jit(solution)/shard_map/all_to_all | solution.py:1036
  241.4 1.3 copy-start
  298.3 8.9 %copy-start.1 = (bf16[985,768]{1,0:T(8,128)(2,1)S(1)}, bf16[985,768]{1,0:T(8,128)(2,1)}, u32[]{:S(2)}) copy-start(bf16[985,768]{1,0:T(8,128)(2,1)} %get-tuple-element.106) | copy-start | bytes 4538884
